TPU v7x, 512 devices: a whole 4x4x16 slice. The times are simulated.
512 devices in a mesh: dp: 16 (over y_lo, x, core), tm: 32 (over y_hi, z).
Axes of the slice: x: 4, y: 4 (y_hi: 2, y_lo: 2; y = y_hi * 2 + y_lo), z: 16, core: 2. Of those that a mesh axis runs over, the one named last changes fastest.
Arguments:
- latent: float32 [16, 64, 16384], P('dp', None, 'tm'), may hold values from -40 to 40
- target: float32 [16, 32768], P('dp', 'tm'), may hold values from -20 to 20
- up_kernel: float32 [4, 32, 64], replicated, may hold values from -0.5 to 0.5
- inner_kernel: float32 [3, 16, 32], replicated, may hold values from -0.625 to 0.625
- outer_kernel: float32 [32, 16], replicated, may hold values from -1.5 to 1.5
- out_kernel: float32 [7, 32], replicated, may hold values from -0.375 to 0.375
Outputs:
- latent_grad: float32 [16, 64, 16384], P('dp', None, 'tm')
- up_update: float32 [4, 32, 64], replicated
- inner_update: float32 [3, 16, 32], replicated
- outer_update: float32 [32, 16], replicated
- out_update: float32 [7, 32], replicated
All inputs are finite; a program needn't handle non-finite values.
Results may differ from a plain program's by a relative error of at most 0.0003.
Values sent between devices are 32-bit elements; how exact they have to be, the bound alone decides.
A program may use at most 64 MiB of HBM per device.

v0:
```python
import functools

import jax
import jax.numpy as jnp
from jax import lax
from jax.sharding import Mesh
from jax.sharding import PartitionSpec as P

MELS = 64
WIN_COARSE = 1024
WIN_FINE = 256
TM = ("tm_0", "tm_1")
DP_TM = ("dp_0", "dp_1", "dp_2", "tm_0", "tm_1")
DP = ("dp_0", "dp_1", "dp_2")


LOSS_WEIGHTS = (0.25, 0.5, 0.5)


def padded_2(cells, sides, width):
    for axis, dim in sides:
        count = lax.axis_size(axis)
        ends = count - 1
        head = lax.slice_in_dim(cells, 0, width, axis=dim)
        tail = lax.slice_in_dim(cells, cells.shape[dim] - width, cells.shape[dim], axis=dim)
        cells = jnp.concatenate(
            [
                lax.ppermute(tail, axis, [(i, (i + 1) % count) for i in range(ends)]),
                cells,
                lax.ppermute(head, axis, [((i + 1) % count, i) for i in range(ends)]),
            ],
            axis=dim,
        )
    return cells


def from_behind(x, axis, by):
    peers = lax.axis_size(axis)
    pairs = [(i, i + by) for i in range(peers) if 0 <= i + by < peers]
    return lax.ppermute(x, axis, pairs)


def sent_to_all(x, axis):
    copies = jnp.broadcast_to(x, (lax.axis_size(axis), *x.shape))
    return lax.all_to_all(copies, axis, split_axis=0, concat_axis=0, tiled=True)


def of_everyone(x, axis):
    everything = sent_to_all(x, axis)
    return jnp.sum(everything, axis=0)


def over_axes(x, axes):
    return functools.reduce(lax.psum, axes, x)


def product(form, left, right):
    return jnp.einsum(
        form, left, right, precision=lax.Precision.HIGHEST, preferred_element_type=jnp.float32
    )


def mel_bank(window, mel_count):
    half_window = window // 2
    top_mel = 2595.0 * jnp.log10(1.0 + 12000.0 / 700.0)
    points = (jnp.arange(mel_count + 1, dtype=jnp.float32) + 1.0) / (mel_count + 2.0) * top_mel
    centers = 700.0 * (jnp.power(10.0, points / 2595.0) - 1.0) / 12000.0 * half_window
    spacing = jnp.maximum(centers[1:] - centers[:-1], 1.0)
    places = jnp.arange(half_window, dtype=jnp.float32)[:, None]
    return jnp.maximum(0.0, 1.0 - jnp.abs(places - centers[None, :mel_count]) / spacing[None, :])


def dft_table(window):
    half_window = window // 2
    sample = jnp.arange(window, dtype=jnp.int32)[:, None]
    freq_index = jnp.arange(half_window, dtype=jnp.int32)[None, :]
    angles = (sample * freq_index % window).astype(jnp.float32) * (2.0 * jnp.pi / window)
    hann_taper = 0.5 - 0.5 * jnp.cos(sample.astype(jnp.float32) * (2.0 * jnp.pi / window))
    return jnp.concatenate([hann_taper * jnp.cos(angles), -hann_taper * jnp.sin(angles)], axis=1)


def framed(signal, window, frame_count):
    hop_size = window // 4
    blocks = signal.reshape(signal.shape[:-1] + (frame_count + 3, hop_size))
    return jnp.concatenate(
        [blocks[..., offset : offset + frame_count, :] for offset in range(4)], axis=-1
    )


def mel_energy(signal, window, frame_count):
    frames = framed(signal, window, frame_count)
    spectra = product("...nf,fk->...nk", frames, dft_table(window))
    half_window = window // 2
    energy = spectra[..., :half_window] ** 2 + spectra[..., half_window:] ** 2
    return product("...nk,km->...nm", energy, mel_bank(window, MELS))


def spectral_loss(signal, target_mel, window, frame_count):
    level = jnp.sqrt(mel_energy(signal, window, frame_count) + 1.0)
    return jnp.sum((level - jnp.sqrt(target_mel + 1.0)) ** 2)


def elu_slope(values):
    return jnp.where(values > 0, 1.0, jnp.exp(jnp.minimum(values, 0.0)))


def apply_mask(values, mask):
    return values * mask


def upsample_forward(values, kernel, stride, previous):
    lagged = jnp.concatenate([previous, values[:, :, :-1]], axis=2)
    phases = product("pij,bjm->bimp", kernel[:stride], values) + product(
        "pij,bjm->bimp", kernel[stride:], lagged
    )
    return (phases.reshape(phases.shape[0], phases.shape[1], -1), lagged)


def taps_forward(padded, kernel, length):
    summed = product("oi,bil->bol", kernel[0], padded[:, :, :length])
    for offset in range(1, kernel.shape[0]):
        summed = summed + product(
            "oi,bil->bol", kernel[offset], padded[:, :, offset : offset + length]
        )
    return summed


def decode_forward(activated, weights, movers, clip_mask):
    up_kernel, inner_kernel, outer_kernel, out_kernel = weights
    lend_frame, border_inner, border_output = movers
    upper, lagged = upsample_forward(activated, up_kernel, 2, lend_frame(activated[:, :, -1:]))
    upper = apply_mask(upper, clip_mask)
    padded_inner = border_inner(jax.nn.elu(upper))
    inner_out = taps_forward(padded_inner, inner_kernel, upper.shape[2])
    hidden = jax.nn.elu(inner_out)
    mixed = apply_mask(upper + product("oi,bil->bol", outer_kernel, hidden), clip_mask)
    padded_output = border_output(jax.nn.elu(mixed))
    waveform = taps_forward(padded_output, out_kernel[:, None, :], upper.shape[2])[:, 0, :]
    return (waveform, (upper, lagged, padded_inner, inner_out, hidden, mixed, padded_output))


def taps_backward(grad_out, padded, kernel, length, keep):
    tap_count = kernel.shape[0]
    row_grad = apply_mask(grad_out, keep)
    kernel_rows = jnp.stack(
        [
            product("nbol,bil->nboi", row_grad, padded[:, :, offset : offset + length])
            for offset in range(tap_count)
        ],
        axis=2,
    )
    spread = jnp.zeros(grad_out.shape[:2] + (kernel.shape[2], length + tap_count - 1), jnp.float32)
    for offset in range(tap_count):
        moved = product("oi,nbol->nbil", kernel[offset], grad_out)
        spread = spread + jnp.pad(moved, ((0, 0), (0, 0), (0, 0), (offset, tap_count - 1 - offset)))
    return (kernel_rows, spread)


def rims_backward(spread, rim_width):
    interior = spread[..., rim_width:-rim_width]
    return interior


def residual_backward(
    grad_mixed, upper, padded, inner_out, hidden, inner_kernel, outer_kernel, keep
):
    length = upper.shape[-1]
    outer_rows = product("nbol,bil->nboi", apply_mask(grad_mixed, keep), hidden)
    grad_inner = product("oi,nbol->nbil", outer_kernel, grad_mixed) * elu_slope(inner_out)
    inner_rows, spread = taps_backward(grad_inner, padded, inner_kernel, length, keep)
    grad_rectified = rims_backward(spread, 1)
    return (grad_mixed + grad_rectified * elu_slope(upper), inner_rows, outer_rows)


def upsample_backward(grad_upper, values, lagged, kernel, stride, keep):
    phase_shape = grad_upper.shape[:3] + (values.shape[-1], stride)
    grad_phase = grad_upper.reshape(phase_shape)
    row_phase = apply_mask(grad_upper, keep).reshape(phase_shape)
    first_rows = product("nbimp,bjm->nbpij", row_phase, values)
    second_rows = product("nbimp,bjm->nbpij", row_phase, lagged)
    grad_values = product("pij,nbimp->nbjm", kernel[:stride], grad_phase)
    grad_lagged = product("pij,nbimp->nbjm", kernel[stride:], grad_phase)
    arrived = jnp.zeros_like(grad_lagged[..., :1])
    grad_values = grad_values + jnp.concatenate([grad_lagged[..., 1:], arrived], axis=-1)
    return (grad_values, jnp.concatenate([first_rows, second_rows], axis=2))


def local(latent, target, up_kernel, inner_kernel, outer_kernel, out_kernel):
    weights = (up_kernel, inner_kernel, outer_kernel, out_kernel)
    samples = target.shape[1]
    frames_here = latent.shape[2]
    latent_in = padded_2(latent, ((TM, 2),), 4)
    start_frame = 4
    margin = 8

    def lend_frame(edge):
        return jnp.zeros_like(edge)

    def border_inner(values):
        return jnp.pad(values, ((0, 0), (0, 0), (1, 1)))

    def border_output(values):
        return jnp.pad(values, ((0, 0), (0, 0), (3, 3)))

    shard_index = lax.axis_index(TM)
    shard_total = lax.axis_size(TM)
    wide_length = samples + 2 * margin
    local_places = jnp.arange(wide_length, dtype=jnp.int32)
    clip_places = samples * shard_index - margin + local_places
    clip_mask = ((clip_places >= 0) & (clip_places < samples * shard_total)).astype(jnp.float32)
    keep_rows = ((local_places >= margin) & (local_places < margin + samples)).astype(jnp.float32)
    activated = jax.nn.elu(latent_in)
    wave_all, saved = decode_forward(
        activated, weights, (lend_frame, border_inner, border_output), clip_mask
    )
    upper, lagged, padded_inner, inner_out, hidden, mixed, padded_output = saved
    waveform = wave_all[:, margin : margin + samples]
    tail_length = 3 * WIN_COARSE // 4
    wave_next, target_next = from_behind(
        (waveform[:, :tail_length], target[:, :tail_length]), TM, -1
    )
    long_wave = jnp.concatenate([waveform, wave_next], axis=1)
    long_target = jnp.concatenate([target, target_next], axis=1)
    gradients = [2.0 * (waveform - target)]
    tails = []
    for window in (WIN_COARSE, WIN_FINE):
        hop_size = window // 4
        frame_count = samples // hop_size
        span = samples + 3 * hop_size
        target_mel = mel_energy(long_target[:, :span], window, frame_count)

        def scale_loss(signal):
            return spectral_loss(signal, target_mel, window, frame_count)

        local_grad = jax.grad(scale_loss)(long_wave[:, :span])
        gradients.append(local_grad[:, :samples])
        tails.append(jnp.pad(local_grad[:, samples:], ((0, 0), (0, tail_length - 3 * hop_size))))
    coarse_in, fine_in = from_behind((tails[0], tails[1]), TM, 1)
    gradients[1] = gradients[1] + jnp.pad(coarse_in, ((0, 0), (0, samples - tail_length)))
    gradients[2] = gradients[2] + jnp.pad(fine_in, ((0, 0), (0, samples - tail_length)))
    squares = jnp.stack([jnp.sum(member * member, axis=1) for member in gradients], axis=1)
    squares = of_everyone(squares, TM)
    total_samples = samples * lax.axis_size(TM)
    grad_scale = jnp.asarray(LOSS_WEIGHTS, jnp.float32)[None, :] / jnp.sqrt(
        squares / total_samples + 1e-06
    )
    streams = jnp.stack(gradients, axis=0)
    row_weights = jnp.transpose(grad_scale)
    streams_wide = padded_2(streams, ((TM, 2),), 8)
    wave_length = mixed.shape[2]
    out_taps = out_kernel[:, None, :]
    kernel_rows_out, spread_out = taps_backward(
        streams_wide[:, :, None, :], padded_output, out_taps, wave_length, keep_rows
    )
    out_rows = kernel_rows_out[:, :, :, 0, :]
    grad_final = rims_backward(spread_out, 3)
    grad_mixed = apply_mask(grad_final * elu_slope(mixed), clip_mask)
    grad_upper, inner_rows, outer_rows = residual_backward(
        grad_mixed, upper, padded_inner, inner_out, hidden, inner_kernel, outer_kernel, keep_rows
    )
    grad_activated, up_rows = upsample_backward(
        apply_mask(grad_upper, clip_mask), activated, lagged, up_kernel, 2, keep_rows
    )
    grad_latent_rows = grad_activated[..., start_frame : start_frame + frames_here] * elu_slope(
        latent
    )
    latent_grad = product("nb,nbcm->bcm", row_weights, grad_latent_rows)
    local_totals = [
        product("nb,nb...->...", row_weights, member)
        for member in (up_rows, inner_rows, outer_rows, out_rows)
    ]
    param_count = sum((member.size for member in local_totals))
    summed = (
        over_axes(local_totals[0], DP_TM),
        over_axes(local_totals[1], DP_TM),
        over_axes(local_totals[2], DP_TM),
        over_axes(local_totals[3], DP_TM),
    )
    squares_all = sum((jnp.sum(member * member) for member in summed))
    factor = jnp.minimum(1.0, 1.0 / jnp.sqrt(squares_all / param_count + 1e-06))
    updates = [member * factor for member in summed]
    return (latent_grad, updates[0], updates[1], updates[2], updates[3])


def solution(mesh):
    torus = Mesh(mesh.devices.reshape(2, 4, 2, 2, 16), ("dp_0", "dp_1", "dp_2", "tm_0", "tm_1"))
    return jax.shard_map(
        local,
        mesh=torus,
        in_specs=(P(DP, None, TM), P(DP, TM), P(), P(), P(), P()),
        out_specs=(P(DP, None, TM), P(), P(), P(), P()),
        check_vma=False,
    )
```

profile of v0, /device:TPU:4, one launch (start us, length us, event | category | flops | bytes accessed | tf_op | source)
XLA Modules:
  0.0 234.9 jit_solution(9888173262925613833)
XLA Ops:
  0.6 1.3 slice.287
  1.9 1.3 collective-permute-start.3
  3.2 0.9 fusion.294
  4.1 4.5 %collective-permute-start = (f32[1,64,4]{2,1,0:T(8,128)S(1)}, f32[1,64,4]{2,1,0:T(8,128)S(1)}, u32[]{:S(2)}, u32[]{:S(2)}) collective-permute-start(f32[1,64,4]{2,1,0:T(8,128)S(1)} %get-tuple-element.33), channel_id=1, source_target_pairs={{0,1},{1,2},{2,3},{3,4},{4,5},{5,6},{6,7},{7,8},{8,9},{9,10},{10,1... | collective-permute-start | bytes 3080 | tf_op jit(solution)/shard_map/ppermute | solution.py:28
  8.6 1.3 collective-permute-start.1
  10.2 1.6 select_bitcast_fusion
  11.7 0.6 fusion.303
  13.0 1.6 slice_bitcast_fusion.6
  14.6 1.2 sine_multiply_fusion.1
  15.8 9.4 %sine_multiply_fusion = (f32[1024,512]{1,0:T(8,128)S(1)}, f32[1024,512]{1,0:T(8,128)}) fusion(f32[1024]{0:T(1024)S(1)} %fusion.227, f32[1024]{0:T(1024)S(1)} %multiply_subtract_fusion), kind=kLoop, calls=%fused_computation.21 | loop fusion | flops 8388608 | bytes 4202496 | tf_op jit(solution)/shard_map/jvp()/mul | solution.py:79
  27.3 1.0 fusion.81
  28.3 1.3 convolution_add_fusion.1
  29.6 1.0 fusion.6
  30.6 0.6 fusion.115
  31.6 1.0 convolution_reduce_fusion.3
  32.6 0.7 fusion.62
  33.3 1.0 convolution_reduce_fusion.2
  34.3 1.0 convolution_reduce_fusion.1
  35.3 1.0 convolution_reduce_fusion
  36.3 1.0 convolution_reduce_fusion.5
  37.3 1.0 convolution_reduce_fusion.4
  38.5 1.0 exponential_select_fusion
  39.6 0.7 multiply_reduce_fusion.6
  40.4 1.9 copy.66
  42.3 1.3 collective-permute-start.2
  43.6 0.7 constant_dynamic-update-slice_fusion
  44.4 3.7 %fusion.15 = f32[1,4,1024]{2,1,0:T(4,128)S(1)} fusion(f32[1024,512]{1,0:T(8,128)S(1)} %get-tuple-element.91, f32[1024,512]{1,0:T(8,128)} %get-tuple-element.92, f32[1,4,256]{2,1,0:T(4,128)S(1)} %get-tuple-element.67, f32[1,4,256]{2,1,0:T(4,128)S(1)} %get-tuple-element.68, f32[1,4,256]{2,1,0:T(4,128)S(1)} %get-tuple-element.69, ...), kind=kOutput, calls=%fused_computation.37 | convolution fusion | flops 51392512 | bytes 4227072 | tf_op jit(solution)/shard_map/...nf,fk->...nk/dot_general | solution.py:58
  50.0 5.3 %collective-permute-start.5 = (f32[1,768]{1,0:T(1,128)S(1)}, f32[1,768]{1,0:T(1,128)S(1)}, u32[]{:S(2)}, u32[]{:S(2)}) collective-permute-start(f32[1,768]{1,0:T(1,128)S(1)} %pad.112), channel_id=1, source_target_pairs={{0,1},{1,2},{2,3},{3,4},{4,5},{5,6},{6,7},{7,8},{8,9},{9,10},{10,1... | collective-permute-start | bytes 9224 | tf_op jit(solution)/shard_map/ppermute | solution.py:40
  55.4 3.7 %fusion.14 = f32[1,4,1024]{2,1,0:T(4,128)S(1)} fusion(f32[1024,512]{1,0:T(8,128)S(1)} %get-tuple-element.91, f32[1024,512]{1,0:T(8,128)} %get-tuple-element.92, f32[1,4,256]{2,1,0:T(4,128)S(1)} %get-tuple-element.71, f32[1,4,256]{2,1,0:T(4,128)S(1)} %get-tuple-element.72, f32[1,4,256]{2,1,0:T(4,128)S(1)} %get-tuple-element.73, ...), kind=kOutput, calls=%fused_computation.36 | convolution fusion | flops 51392512 | bytes 4227072 | tf_op jit(solution)/shard_map/jvp(...nf,fk->...nk)/dot_general | solution.py:58
  60.7 3.5 %fusion.16 = f32[1,4,1024]{2,1,0:T(4,128)S(1)} fusion(f32[1024,512]{1,0:T(8,128)S(1)} %get-tuple-element.91, f32[1024,512]{1,0:T(8,128)S(1)} %copy-done.1, f32[1,4,512]{2,1,0:T(4,128)S(1)} %get-tuple-element.36, f32[1,4,512]{2,1,0:T(4,128)S(1)} %get-tuple-element.35), kind=kOutput, calls=%fused_computation.38 | convolution fusion | flops 51384320 | bytes 4227072 | tf_op jit(solution)/shard_map/transpose(jvp(...nf,fk->...nk))/dot_general | solution.py:58
  64.3 3.9 %collective-permute-start.4 = (f32[1,768]{1,0:T(1,128)S(1)}, f32[1,768]{1,0:T(1,128)S(1)}, u32[]{:S(2)}, u32[]{:S(2)}) collective-permute-start(f32[1,768]{1,0:T(1,128)S(1)} %slice.335), channel_id=1, source_target_pairs={{0,1},{1,2},{2,3},{3,4},{4,5},{5,6},{6,7},{7,8},{8,9},{9,10},{10,1... | collective-permute-start | bytes 9224 | tf_op jit(solution)/shard_map/ppermute | solution.py:40
  68.9 0.7 collective-permute-done.4
  70.3 1.3 collective-permute-start.7
  71.6 5.5 %collective-permute-start.6 = (f32[3,1,8]{2,1,0:T(1,128)S(1)}, f32[3,1,8]{2,1,0:T(1,128)S(1)}, u32[]{:S(2)}, u32[]{:S(2)}) collective-permute-start(f32[3,1,8]{2,1,0:T(1,128)S(1)} %get-tuple-element.55), channel_id=1, source_target_pairs={{0,1},{1,2},{2,3},{3,4},{4,5},{5,6},{6,7},{7,8},{8,9},{9,10},{10,1... | collective-permute-start | bytes 296 | tf_op jit(solution)/shard_map/ppermute | solution.py:28
  77.0 2.0 maximum_bitcast_fusion.10
  79.1 0.6 broadcast_in_dim.24
  79.7 21.7 %all-to-all-start = ((f32[32,1,3]{2,1,0:T(1,128)}), f32[32,1,3]{2,1,0:T(1,128)}, u32[]{:S(2)}, u32[]{:S(2)}) async-start(f32[32,1,3]{2,1,0:T(1,128)} %broadcast_in_dim.24), calls=%async_computation | async-start | bytes 32768 | tf_op jit(solution)/shard_map/all_to_all | solution.py:45
  101.6 0.9 convolution_bitcast_fusion.21
  102.4 0.9 convolution_bitcast_fusion.18
  103.3 0.9 convolution_bitcast_fusion.19
  104.2 0.9 convolution_bitcast_fusion.20
  105.1 0.9 convolution_bitcast_fusion.22
  106.0 0.9 convolution_bitcast_fusion.23
  106.9 0.9 convolution_bitcast_fusion.24
  108.4 0.8 fusion.33
  109.2 1.5 convolution_bitcast_fusion.10
  111.1 1.0 convolution_bitcast_fusion.11
  112.1 1.0 convolution_bitcast_fusion.12
  115.6 0.8 copy.71
  116.4 2.2 convolution_bitcast_fusion.7
  118.6 1.4 convolution_bitcast_fusion.8
  120.5 0.8 copy.68
  123.8 0.8 reduce_sum.75
  125.3 0.6 fusion.39
  125.9 9.4 %all-reduce.33 = (f32[4,32,64]{2,1,0:T(8,128)S(1)}, f32[3,16,32]{2,1,0:T(8,128)S(1)}, f32[32,16]{0,1:T(8,128)S(1)}, f32[7,32]{1,0:T(8,128)S(1)}) all-reduce(f32[4,32,64]{2,1,0:T(8,128)S(1)} %bitcast.456, f32[3,16,32]{2,1,0:T(8,128)S(1)} %bitcast.461, ...), channel_id=1, replica_groups=mesh['dp_0'=2,'dp_1'=4,'dp_2'=2,'tm_0'=2,'tm_1'=16] {'dp_0'}, use_global_device_ids=true, to_apply=%region_4.5 | all-reduce | flops 10464 | bytes 83712 | tf_op jit(solution)/shard_map/psum | solution.py:54
  135.4 16.7 %all-reduce.30 = (f32[4,32,64]{2,1,0:T(8,128)S(1)}, f32[3,16,32]{2,1,0:T(8,128)S(1)}, f32[32,16]{0,1:T(8,128)S(1)}, f32[7,32]{1,0:T(8,128)S(1)}) all-reduce(f32[4,32,64]{2,1,0:T(8,128)S(1)} %get-tuple-element.21, f32[3,16,32]{2,1,0:T(8,128)S(1)} %get-tuple-element.22, ...), channel_id=1, replica_groups=mesh['dp_0'=2,'dp_1'=4,'dp_2'=2,'tm_0'=2,'tm_1'=16] {'dp_1'}, use_global_device_ids=true, to_apply=%region_5.6 | all-reduce | flops 10464 | bytes 83712 | tf_op jit(solution)/shard_map/psum | solution.py:54
  152.1 3.7 %all-reduce.32 = (f32[4,32,64]{2,1,0:T(8,128)S(1)}, f32[3,16,32]{2,1,0:T(8,128)S(1)}, f32[32,16]{0,1:T(8,128)S(1)}, f32[7,32]{1,0:T(8,128)S(1)}) all-reduce(f32[4,32,64]{2,1,0:T(8,128)S(1)} %get-tuple-element.9, f32[3,16,32]{2,1,0:T(8,128)S(1)} %get-tuple-element.10, ...), channel_id=1, replica_groups=mesh['dp_0'=2,'dp_1'=4,'dp_2'=2,'tm_0'=2,'tm_1'=16] {'dp_2'}, use_global_device_ids=true, to_apply=%region_6.7 | all-reduce | flops 10464 | bytes 83712 | tf_op jit(solution)/shard_map/psum | solution.py:54
  155.8 12.9 %all-reduce.31 = (f32[4,32,64]{2,1,0:T(8,128)S(1)}, f32[3,16,32]{2,1,0:T(8,128)S(1)}, f32[32,16]{0,1:T(8,128)S(1)}, f32[7,32]{1,0:T(8,128)S(1)}) all-reduce(f32[4,32,64]{2,1,0:T(8,128)S(1)} %get-tuple-element.17, f32[3,16,32]{2,1,0:T(8,128)S(1)} %get-tuple-element.18, ...), channel_id=1, replica_groups=mesh['dp_0'=2,'dp_1'=4,'dp_2'=2,'tm_0'=2,'tm_1'=16] {'tm_0'}, use_global_device_ids=true, to_apply=%region_7.8 | all-reduce | flops 10464 | bytes 83712 | tf_op jit(solution)/shard_map/psum | solution.py:54
  168.8 56.8 %all-reduce.29 = (f32[4,32,64]{2,1,0:T(8,128)S(1)}, f32[3,16,32]{2,1,0:T(8,128)S(1)}, f32[32,16]{0,1:T(8,128)S(1)}, f32[7,32]{1,0:T(8,128)S(1)}) all-reduce(f32[4,32,64]{2,1,0:T(8,128)S(1)} %get-tuple-element.13, f32[3,16,32]{2,1,0:T(8,128)S(1)} %get-tuple-element.14, ...), channel_id=1, replica_groups=mesh['dp_0'=2,'dp_1'=4,'dp_2'=2,'tm_0'=2,'tm_1'=16] {'tm_1'}, use_global_device_ids=true, to_apply=%region_8.9 | all-reduce | flops 10464 | bytes 83712 | tf_op jit(solution)/shard_map/psum | solution.py:54
  227.4 0.6 multiply_reduce_fusion
  231.8 0.6 broadcast_multiply_fusion.2
  232.5 0.6 broadcast_multiply_fusion.1
  233.1 1.2 fusion.27
  234.3 0.7 copy.79
  (187 shorter events, 18.3 us)
Async XLA Ops:
  0.6 30.7 %copy-start = (f32[32,16]{0,1:T(8,128)S(1)}, f32[32,16]{0,1:T(8,128)}, u32[]{:S(2)}) copy-start(f32[32,16]{0,1:T(8,128)} %param.11) | copy-start | bytes 6148
  1.9 41.6 %collective-permute-start.3 = (f32[1,768]{1,0:T(1,128)}, f32[1,768]{1,0:T(1,128)}, u32[]{:S(2)}, u32[]{:S(2)}) collective-permute-start(f32[1,768]{1,0:T(1,128)} %slice.287), channel_id=1, source_target_pairs={{1,0},{2,1},{3,2},{4,3},{5,4},{6,5},{7,6},{8,7},{9,8},{10,9},{11,1... | collective-permute-start | bytes 9224 | tf_op jit(solution)/shard_map/ppermute | solution.py:40
  4.1 21.2 %collective-permute-start = (f32[1,64,4]{2,1,0:T(8,128)S(1)}, f32[1,64,4]{2,1,0:T(8,128)S(1)}, u32[]{:S(2)}, u32[]{:S(2)}) collective-permute-start(f32[1,64,4]{2,1,0:T(8,128)S(1)} %get-tuple-element.33), channel_id=1, source_target_pairs={{0,1},{1,2},{2,3},{3,4},{4,5},{5,6},{6,7},{7,8},{8,9},{9,10},{10,1... | collective-permute-start | bytes 3080 | tf_op jit(solution)/shard_map/ppermute | solution.py:28
  8.6 16.7 %collective-permute-start.1 = (f32[1,64,4]{2,1,0:T(8,128)S(1)}, f32[1,64,4]{2,1,0:T(8,128)S(1)}, u32[]{:S(2)}, u32[]{:S(2)}) collective-permute-start(f32[1,64,4]{2,1,0:T(8,128)S(1)} %get-tuple-element.34), channel_id=1, source_target_pairs={{1,0},{2,1},{3,2},{4,3},{5,4},{6,5},{7,6},{8,7},{9,8},{10,9},{11,1... | collective-permute-start | bytes 3080 | tf_op jit(solution)/shard_map/ppermute | solution.py:30
  15.8 9.5 %copy-start.4 = (f32[1,64,512]{2,1,0:T(8,128)S(1)}, f32[1,64,512]{2,1,0:T(8,128)}, u32[]{:S(2)}) copy-start(f32[1,64,512]{2,1,0:T(8,128)} %param.7) | copy-start | bytes 393220
  15.8 9.5 %copy-start.15 = (f32[4,32,64]{2,1,0:T(8,128)S(1)}, f32[4,32,64]{2,1,0:T(8,128)}, u32[]{:S(2)}) copy-start(f32[4,32,64]{2,1,0:T(8,128)} %param.9) | copy-start | bytes 98308
  25.3 1.8 copy-start.18
  25.3 1.8 copy-start.19
  25.9 0.7 copy-start.6
  27.3 11.0 %copy-start.14 = (f32[7,32]{1,0:T(8,128)S(1)}, f32[7,32]{1,0:T(8,128)}, u32[]{:S(2)}) copy-start(f32[7,32]{1,0:T(8,128)} %param.12) | copy-start | bytes 2692
  28.3 11.3 %copy-start.24 = (f32[1,1024]{1,0:T(1,128)S(1)}, f32[1,1024]{1,0:T(1,128)}, u32[]{:S(2)}) copy-start(f32[1,1024]{1,0:T(1,128)} %param.8) | copy-start | bytes 12292
  31.6 1.0 copy-start.9
  42.3 6.2 %collective-permute-start.2 = (f32[1,768]{1,0:T(1,128)S(1)}, f32[1,768]{1,0:T(1,128)S(1)}, u32[]{:S(2)}, u32[]{:S(2)}) collective-permute-start(f32[1,768]{1,0:T(1,128)S(1)} %slice.321), channel_id=1, source_target_pairs={{1,0},{2,1},{3,2},{4,3},{5,4},{6,5},{7,6},{8,7},{9,8},{10,9},{11,1... | collective-permute-start | bytes 9224 | tf_op jit(solution)/shard_map/ppermute | solution.py:40
  44.4 3.8 %copy-start.2 = (f32[256,128]{1,0:T(8,128)S(1)}, f32[256,128]{1,0:T(8,128)}, u32[]{:S(2)}) copy-start(f32[256,128]{1,0:T(8,128)} %get-tuple-element.89) | copy-start | bytes 393220
  44.4 3.8 %copy-start.3 = (f32[256,128]{1,0:T(8,128)S(1)}, f32[256,128]{1,0:T(8,128)}, u32[]{:S(2)}) copy-start(f32[256,128]{1,0:T(8,128)} %get-tuple-element.90) | copy-start | bytes 393220
  44.4 4.5 %copy-start.41 = (f32[64]{0:T(128)S(1)}, f32[64]{0:T(128)}, u32[]{:S(2)}) copy-start(f32[64]{0:T(128)} %get-tuple-element.85) | copy-start | bytes 772
  44.4 4.5 %copy-start.42 = (f32[64]{0:T(128)S(1)}, f32[64]{0:T(128)}, u32[]{:S(2)}) copy-start(f32[64]{0:T(128)} %get-tuple-element.86) | copy-start | bytes 772
  50.0 18.2 %collective-permute-start.5 = (f32[1,768]{1,0:T(1,128)S(1)}, f32[1,768]{1,0:T(1,128)S(1)}, u32[]{:S(2)}, u32[]{:S(2)}) collective-permute-start(f32[1,768]{1,0:T(1,128)S(1)} %pad.112), channel_id=1, source_target_pairs={{0,1},{1,2},{2,3},{3,4},{4,5},{5,6},{6,7},{7,8},{8,9},{9,10},{10,1... | collective-permute-start | bytes 9224 | tf_op jit(solution)/shard_map/ppermute | solution.py:40
  55.4 3.7 %copy-start.39 = (f32[64]{0:T(128)S(1)}, f32[64]{0:T(128)}, u32[]{:S(2)}) copy-start(f32[64]{0:T(128)} %get-tuple-element.83) | copy-start | bytes 772
  55.4 3.7 %copy-start.40 = (f32[64]{0:T(128)S(1)}, f32[64]{0:T(128)}, u32[]{:S(2)}) copy-start(f32[64]{0:T(128)} %get-tuple-element.84) | copy-start | bytes 772
  59.1 1.6 copy-start.1
  60.7 40.9 %copy-start.10 = (f32[1,32,1040]{2,1,0:T(8,128)S(1)}, f32[1,32,1040]{2,1,0:T(8,128)}, u32[]{:S(2)}) copy-start(f32[1,32,1040]{2,1,0:T(8,128)} %copy-done.9) | copy-start | bytes 399364
  60.7 47.3 %copy-start.31 = (f32[32]{0:T(128)S(1)}, f32[32]{0:T(128)}, u32[]{:S(2)}) copy-start(f32[32]{0:T(128)} %get-tuple-element.76) | copy-start | bytes 388
  60.7 47.3 %copy-start.32 = (f32[32]{0:T(128)S(1)}, f32[32]{0:T(128)}, u32[]{:S(2)}) copy-start(f32[32]{0:T(128)} %get-tuple-element.77) | copy-start | bytes 388
  60.7 47.3 %copy-start.33 = (f32[32]{0:T(128)S(1)}, f32[32]{0:T(128)}, u32[]{:S(2)}) copy-start(f32[32]{0:T(128)} %get-tuple-element.78) | copy-start | bytes 388
  60.7 47.3 %copy-start.34 = (f32[32]{0:T(128)S(1)}, f32[32]{0:T(128)}, u32[]{:S(2)}) copy-start(f32[32]{0:T(128)} %get-tuple-element.79) | copy-start | bytes 388
  60.7 47.3 %copy-start.35 = (f32[32]{0:T(128)S(1)}, f32[32]{0:T(128)}, u32[]{:S(2)}) copy-start(f32[32]{0:T(128)} %get-tuple-element.80) | copy-start | bytes 388
  60.7 47.3 %copy-start.36 = (f32[32]{0:T(128)S(1)}, f32[32]{0:T(128)}, u32[]{:S(2)}) copy-start(f32[32]{0:T(128)} %get-tuple-element.81) | copy-start | bytes 388
  60.7 47.3 %copy-start.37 = (f32[32]{0:T(128)S(1)}, f32[32]{0:T(128)}, u32[]{:S(2)}) copy-start(f32[32]{0:T(128)} %get-tuple-element.82) | copy-start | bytes 388
  64.3 5.2 %collective-permute-start.4 = (f32[1,768]{1,0:T(1,128)S(1)}, f32[1,768]{1,0:T(1,128)S(1)}, u32[]{:S(2)}, u32[]{:S(2)}) collective-permute-start(f32[1,768]{1,0:T(1,128)S(1)} %slice.335), channel_id=1, source_target_pairs={{0,1},{1,2},{2,3},{3,4},{4,5},{5,6},{6,7},{7,8},{8,9},{9,10},{10,1... | collective-permute-start | bytes 9224 | tf_op jit(solution)/shard_map/ppermute | solution.py:40
  70.3 31.1 %collective-permute-start.7 = (f32[3,1,8]{2,1,0:T(1,128)S(1)}, f32[3,1,8]{2,1,0:T(1,128)S(1)}, u32[]{:S(2)}, u32[]{:S(2)}) collective-permute-start(f32[3,1,8]{2,1,0:T(1,128)S(1)} %get-tuple-element.54), channel_id=1, source_target_pairs={{1,0},{2,1},{3,2},{4,3},{5,4},{6,5},{7,6},{8,7},{9,8},{10,9},{11,1... | collective-permute-start | bytes 296 | tf_op jit(solution)/shard_map/ppermute | solution.py:30
  71.6 29.8 %collective-permute-start.6 = (f32[3,1,8]{2,1,0:T(1,128)S(1)}, f32[3,1,8]{2,1,0:T(1,128)S(1)}, u32[]{:S(2)}, u32[]{:S(2)}) collective-permute-start(f32[3,1,8]{2,1,0:T(1,128)S(1)} %get-tuple-element.55), channel_id=1, source_target_pairs={{0,1},{1,2},{2,3},{3,4},{4,5},{5,6},{6,7},{7,8},{8,9},{9,10},{10,1... | collective-permute-start | bytes 296 | tf_op jit(solution)/shard_map/ppermute | solution.py:28
  79.7 44.1 %all-to-all-start = ((f32[32,1,3]{2,1,0:T(1,128)}), f32[32,1,3]{2,1,0:T(1,128)}, u32[]{:S(2)}, u32[]{:S(2)}) async-start(f32[32,1,3]{2,1,0:T(1,128)} %broadcast_in_dim.24), calls=%async_computation | async-start | bytes 32768 | tf_op jit(solution)/shard_map/all_to_all | solution.py:45
  102.4 6.0 %copy-start.7 = (f32[32,1040]{1,0:T(8,128)S(1)}, f32[32,1040]{1,0:T(8,128)}, u32[]{:S(2)}) copy-start(f32[32,1040]{1,0:T(8,128)} %get-tuple-element.31) | copy-start | bytes 399364
  108.4 2.3 copy-start.13
  108.4 4.7 %copy-start.20 = (f32[3,16,32]{2,1,0:T(8,128)S(1)}, f32[3,16,32]{2,1,0:T(8,128)}, u32[]{:S(2)}) copy-start(f32[3,16,32]{2,1,0:T(8,128)} %param.10) | copy-start | bytes 18436
  109.2 5.6 %copy-start.8 = (f32[32,1040]{1,0:T(8,128)S(1)}, f32[32,1040]{1,0:T(8,128)}, u32[]{:S(2)}) copy-start(f32[32,1040]{1,0:T(8,128)} %copy.66) | copy-start | bytes 399364
  115.1 3.4 %copy-start.5 = (f32[1,64,512]{2,1,0:T(8,128)S(1)}, f32[1,64,512]{2,1,0:T(8,128)}, u32[]{:S(2)}) copy-start(f32[1,64,512]{2,1,0:T(8,128)} %param.7) | copy-start | bytes 393220
  120.0 1.3 copy-start.16
  121.3 2.0 copy-start.12
  121.3 2.0 copy-start.11
  121.9 1.7 copy-start.21
  121.9 1.7 copy-start.22
  122.5 1.1 copy-start.38
  122.5 1.1 copy-start.30
  122.5 1.1 copy-start.29
  122.5 1.1 copy-start.28
  122.6 1.2 copy-start.26
  122.6 1.2 copy-start.27
  122.6 1.2 copy-start.25
  122.6 2.0 copy-start.23
  122.6 2.2 copy-start.17
where the time goes:
time: 236 us; the launch traced here: 235 us
  blocking collectives  99.6 us (42%)
  starting transfers between devices  46.1 us (20%)
  matrix products  43.4 us (18%)
  other arithmetic  27.8 us (12%)
  local copies, waits for them, and re-layouts  12.7 us (5%)
  between operations  4.54 us (2%)
    psum x5, blocking collectives, over_axes(): return functools.reduce(lax.psum, axes, x)  99.6 us
    dot_general x49, matrix products, product(): jnp.einsum(form, left, right, precision=lax.Precision.HIGHEST, preferred_...  43.4 us
    all_to_all x1, starting transfers between devices, sent_to_all(): return lax.all_to_all(copies, axis, split_axis=0, concat_axis=0, tiled=True)  21.7 us
    ppermute x4, starting transfers between devices, from_behind(): return lax.ppermute(x, axis, pairs)  11.8 us
    mul x2, other arithmetic, dft_table(): -hann_taper * jnp.sin(angles)  10.7 us
    ppermute x2, starting transfers between devices, padded_2(): lax.ppermute(tail, axis, [(i, (i + 1) % count) for i in range(ends)])  10 us
  transfers between devices with their start and end apart: 9, of which 1 were waited for; matrix products, arithmetic and copies ran while one was open for 30% of the time, Pallas kernels for 0%

commit v1 on v0

v1 whole, which is shorter than its diff:
```python
import functools

import jax
import jax.numpy as jnp
import ml_dtypes
import numpy as np
from jax import lax
from jax.experimental import pallas as pl
from jax.experimental.pallas import tpu as pltpu
from jax.sharding import PartitionSpec as P

F32 = jnp.float32
BF16 = jnp.bfloat16
MESH = pl.DeviceIdType.MESH
MELS = 64
COEFFS = (0.25, 0.5, 0.5)
PARAMS = 10464
Y_HI = 2
TILES = 11


def mel_bank(window):
    half = window // 2
    top = 2595.0 * np.log10(1.0 + 12000.0 / 700.0)
    points = (np.arange(MELS + 1) + 1.0) / (MELS + 2.0) * top
    centers = 700.0 * (np.power(10.0, points / 2595.0) - 1.0) / 12000.0 * half
    spacing = np.maximum(centers[1:] - centers[:-1], 1.0)
    places = np.arange(half)[:, None]
    return np.maximum(0.0, 1.0 - np.abs(places - centers[None, :MELS]) / spacing[None, :])


def halves(x):
    high = x.astype(ml_dtypes.bfloat16)
    low = (x - high.astype(np.float64)).astype(ml_dtypes.bfloat16)
    return high, low


@functools.cache
def tables():
    lane = np.arange(256)
    place = np.where(lane < 128, 2 * lane, 2 * (lane - 128) + 1)

    def waves(bins, window):
        angle = 2.0 * np.pi * ((place[:, None] * bins[None, :]) % window) / window
        return np.cos(angle), np.sin(angle)

    p = np.arange(128)
    cos0, sin0 = waves(4 * p, 1024)
    cos2, sin2 = waves(4 * p + 2, 1024)
    cos1, sin1 = waves(4 * p + 1, 1024)
    cos3, sin3 = waves(4 * p + 3, 1024)
    t0 = np.concatenate([cos0, -sin0], axis=1)
    t2 = np.concatenate([cos2, -sin2], axis=1)
    real = np.concatenate(
        [np.concatenate([cos1, cos3], axis=1), np.concatenate([-sin1, sin3], axis=1)], axis=0
    )
    imag = np.concatenate(
        [np.concatenate([-sin1, -sin3], axis=1), np.concatenate([-cos1, cos3], axis=1)], axis=0
    )
    cosf, sinf = waves(p, 256)
    fine = np.concatenate([cosf, -sinf], axis=1)
    high, low = halves(np.concatenate([t0, t2, real, imag], axis=0))
    fine_high, fine_low = halves(fine)
    move = np.zeros((256, 256))
    move[place, lane] = 1.0
    dft = np.concatenate(
        [high, low, fine_high, fine_low, move.astype(ml_dtypes.bfloat16)], axis=0
    )
    order = np.concatenate([4 * p, 4 * p + 2, 4 * p + 1, 4 * p + 3])
    mels = np.concatenate([mel_bank(1024)[order], mel_bank(256)], axis=0)
    mels = np.concatenate(halves(mels), axis=1)
    taper = 0.5 - 0.5 * np.cos(2.0 * np.pi * (np.arange(4)[:, None] * 256 + place) / 1024)
    taper_fine = 0.5 - 0.5 * np.cos(2.0 * np.pi * place[None, :] / 256)
    tapers = np.concatenate([taper, taper_fine, np.zeros((3, 256))], axis=0).astype(np.float32)
    return dft, mels, tapers


HIGH, LOW, FINE_HIGH, FINE_LOW, MOVE, ROWS = 0, 1536, 3072, 3328, 3584, 3840


def split(x):
    high = x.astype(BF16)
    return high, (x - high.astype(F32)).astype(BF16)


def dot(a, b):
    return lax.dot_general(a, b, (((1,), (0,)), ((), ())), preferred_element_type=F32)


def dot_nt(a, b):
    return lax.dot_general(a, b, (((1,), (1,)), ((), ())), preferred_element_type=F32)


def weight_dot(w, x):
    high, low = w
    m = high.shape[0]
    xh, xl = split(x)
    both = dot(jnp.concatenate([high, low], axis=0), xh)
    return both[:m] + both[m:] + dot(high, xl)


def rows_dot(x, high, low, product=dot):
    m = x.shape[0]
    xh, xl = split(x)
    both = product(jnp.concatenate([xh, xl], axis=0), high)
    return both[:m] + both[m:] + product(xh, low)


def gram(a, b):
    m = a.shape[0]
    ah, al = split(a)
    bh, bl = split(b)
    both = dot_nt(jnp.concatenate([ah, al], axis=0), bh)
    return both[:m] + both[m:] + dot_nt(ah, bl)


def elu_and_slope(x):
    slope = jnp.exp(jnp.minimum(x, 0.0))
    return jnp.maximum(x, 0.0) + (slope - 1.0), slope


def roll(x, by, axis=1):
    return pltpu.roll(x, by % x.shape[axis], axis)


def coarse_spectrum(blocks, tapers, table):
    x = [blocks[b : b + 16, :] * tapers[b : b + 1, :] for b in range(4)]
    even, odd = x[0] + x[2], x[1] + x[3]
    cross = jnp.concatenate([x[0] - x[2], x[1] - x[3]], axis=1)
    return (
        rows_dot(even + odd, table[HIGH : HIGH + 256, :], table[LOW : LOW + 256, :]),
        rows_dot(even - odd, table[HIGH + 256 : HIGH + 512, :], table[LOW + 256 : LOW + 512, :]),
        rows_dot(cross, table[HIGH + 512 : HIGH + 1024, :], table[LOW + 512 : LOW + 1024, :]),
        rows_dot(cross, table[HIGH + 1024 : HIGH + 1536, :], table[LOW + 1024 : LOW + 1536, :]),
    )


def coarse_energy(parts):
    s0, s2, re, im = (part * part for part in parts)
    return jnp.concatenate(
        [s0[:, :128] + s0[:, 128:], s2[:, :128] + s2[:, 128:], re + im], axis=1
    )


def fine_frames(blocks, tapers):
    now, later = blocks[3:11, :], blocks[4:12, :]
    lane = lax.broadcasted_iota(jnp.int32, (8, 128), 1)
    frames = [now]
    for d in range(1, 4):
        keep = lane < 128 - 32 * d
        frames.append(
            jnp.concatenate(
                [
                    jnp.where(
                        keep,
                        roll(now[:, s : s + 128], -32 * d),
                        roll(later[:, s : s + 128], -32 * d),
                    )
                    for s in (0, 128)
                ],
                axis=1,
            )
        )
    return jnp.concatenate(frames, axis=0) * tapers[4:5, :]


def fine_spectrum(blocks, tapers, table):
    return rows_dot(
        fine_frames(blocks, tapers),
        table[FINE_HIGH : FINE_HIGH + 256, :],
        table[FINE_LOW : FINE_LOW + 256, :],
    )


def level_of(energy, bank):
    m = energy.shape[0]
    eh, el = split(energy)
    both = dot(jnp.concatenate([eh, el], axis=0), bank)
    both = both[:m] + both[m:]
    return jnp.sqrt(both + roll(both, MELS) + 1.0)


def energy_slope(level, target_level, valid, bank):
    m = level.shape[0]
    slope = jnp.where(valid, 1.0 - target_level / level, 0.0)
    sh, sl = split(slope)
    both = dot_nt(jnp.concatenate([sh, sl], axis=0), bank)
    return 2.0 * (both[:m] + both[m:])


def kernel(
    n_dp,
    n_tm,
    latent_hbm,
    target_hbm,
    up_hbm,
    inner_hbm,
    outer_hbm,
    out_hbm,
    dft_hbm,
    mels_hbm,
    tapers_hbm,
    grad_hbm,
    up_ref,
    inner_ref,
    outer_ref,
    out_ref,
    latent,
    halo,
    target_rows,
    up_k,
    inner_k,
    outer_k,
    out_k,
    table,
    mels,
    tapers,
    natural,
    target_blocks,
    wave_tiles,
    wave_blocks,
    frame_grads,
    grad_blocks,
    squares,
    packed,
    plane_rows,
    ring_rows,
    total,
    grad_out,
    load_sem,
    near_send,
    near_recv,
    far_send,
    far_recv,
    store_sem,
):
    dp = lax.axis_index("dp")
    tm = lax.axis_index("tm")
    n_z = n_tm // Y_HI
    n_plane = n_dp * Y_HI
    y_hi = tm // n_z
    z = lax.rem(tm, n_z)
    plane = y_hi * n_dp + dp
    right = lax.rem(tm + 1, n_tm)
    left = lax.rem(tm + n_tm - 1, n_tm)
    other = lax.rem(y_hi + 1, Y_HI) * n_z + z
    first = tm == 0
    last = tm == n_tm - 1

    barrier = pltpu.get_barrier_semaphore()

    def greet(device):
        pl.semaphore_signal(barrier, inc=1, device_id=device, device_id_type=MESH)

    @pl.loop(1, n_tm)
    def _(i):
        greet((dp, lax.rem(tm + i, n_tm)))

    @pl.loop(1, n_dp)
    def _(i):
        peer = lax.rem(dp + i, n_dp)
        greet((peer, tm))
        greet((peer, other))

    loads = [
        pltpu.make_async_copy(source, place, load_sem.at[i])
        for i, (source, place) in enumerate(
            [
                (latent_hbm.at[0], latent),
                (target_hbm, target_rows.at[1]),
                (up_hbm, up_k),
                (inner_hbm, inner_k),
                (outer_hbm, outer_k),
                (out_hbm, out_k),
                (dft_hbm, table),
                (mels_hbm, mels),
                (tapers_hbm, tapers),
            ]
        )
    ]
    for load in loads:
        load.start()
    frames = latent.shape[1]
    wide = frames + 128

    loads[2].wait()
    loads[3].wait()
    loads[4].wait()
    loads[5].wait()
    up_rows = up_k[...]
    up_all = jnp.concatenate([up_rows[r] for r in range(4)], axis=0)
    up_w = jnp.concatenate(
        [
            jnp.concatenate([up_rows[0], up_rows[2]], axis=1),
            jnp.concatenate([up_rows[1], up_rows[3]], axis=1),
        ],
        axis=0,
    )
    up_fwd = split(up_w)
    up_bwd = split(up_all.T)
    taps = jnp.concatenate(
        [inner_k[0], inner_k[1], inner_k[2], jnp.zeros((16, 32), F32)], axis=1
    )
    inner_w = jnp.concatenate([taps, roll(taps, 32)], axis=0)
    inner_fwd = split(inner_w)
    zero = jnp.zeros((16, 32), F32)
    k0, k1, k2 = inner_k[0], inner_k[1], inner_k[2]
    inner_t = jnp.concatenate(
        [
            jnp.concatenate([k1, k2], axis=1),
            jnp.concatenate([k0, k1], axis=1),
            jnp.concatenate([k2, zero], axis=1),
            jnp.concatenate([zero, k0], axis=1),
        ],
        axis=0,
    )
    inner_bwd = split(inner_t.T)
    outer_t = outer_k[...]
    outer_w = jnp.concatenate(
        [jnp.concatenate([outer_t, zero], axis=1), jnp.concatenate([zero, outer_t], axis=1)],
        axis=0,
    )
    outer_bwd = split(outer_w)
    outer_fwd = split(outer_w.T)
    pad = jnp.zeros((1, 32), F32)
    taps_out = out_k[...]
    out_w = jnp.concatenate(
        [
            jnp.concatenate([pad, taps_out], axis=0),
            jnp.concatenate([taps_out, pad], axis=0),
        ],
        axis=1,
    )
    out_w16 = jnp.concatenate([out_w, jnp.zeros((8, 64), F32)], axis=0)
    out_fwd = split(out_w16)
    out_bwd = split(out_w16.T)

    pl.semaphore_wait(barrier, n_tm - 1 + 2 * (n_dp - 1))

    def send(source, place, slot, device):
        copy = pltpu.make_async_remote_copy(
            src_ref=source,
            dst_ref=place,
            send_sem=near_send.at[slot],
            recv_sem=near_recv.at[slot],
            device_id=device,
            device_id_type=MESH,
        )
        copy.start()
        return copy

    near = [
        send(latent_hbm.at[0, :, pl.ds(frames - 128, 128)], halo.at[0], 0, (dp, right)),
        send(latent_hbm.at[0, :, pl.ds(0, 128)], halo.at[1], 1, (dp, left)),
        send(target_hbm, target_rows.at[0], 2, (dp, right)),
        send(target_hbm, target_rows.at[2], 3, (dp, left)),
    ]

    lane = lax.broadcasted_iota(jnp.int32, (1, wide), 1)
    inside = (
        (lane < frames)
        | ((lane < frames + 4) & jnp.logical_not(last))
        | ((lane >= wide - 4) & jnp.logical_not(first))
    )

    loads[0].wait()
    near[0].wait_recv()
    near[1].wait_recv()
    spot = lax.broadcasted_iota(jnp.int32, (64, 128), 1)
    rim = jnp.where(
        (spot < 4) & jnp.logical_not(last),
        halo[1],
        jnp.where((spot >= 124) & jnp.logical_not(first), halo[0], 0.0),
    )
    activated, slope_in = elu_and_slope(jnp.concatenate([latent[...], rim], axis=1))
    stacked = jnp.concatenate([activated, roll(activated, 1)], axis=0)
    upper = jnp.where(inside, weight_dot(up_fwd, stacked), 0.0)
    lifted, slope_upper = elu_and_slope(upper)
    even, odd = lifted[:32], lifted[32:]
    tapped = jnp.concatenate([roll(odd, 1), even, odd, roll(even, -1)], axis=0)
    hidden, slope_inner = elu_and_slope(weight_dot(inner_fwd, tapped))
    mixed = jnp.where(inside, upper + weight_dot(outer_fwd, hidden), 0.0)
    final, slope_mixed = elu_and_slope(mixed)
    taps_8 = weight_dot(out_fwd, final)[:8]
    row = lax.broadcasted_iota(jnp.int32, (8, wide), 0)
    moves = ((2, 0, 0), (1, 1, 2), (-1, 5, 6), (-2, 7, 7))
    aligned = taps_8
    for by, low, high in moves:
        aligned = jnp.where((row >= low) & (row <= high), roll(taps_8, by), aligned)
    aligned = aligned[:, :frames]
    aligned = aligned + roll(aligned, 4, 0)
    aligned = aligned + roll(aligned, 2, 0)
    is_even = lax.rem(row[:, :frames], 2) == 0
    swapped = roll(aligned, 1, 0)
    wave_even = jnp.where(is_even, aligned, swapped)
    wave_odd = jnp.where(is_even, swapped, aligned)
    tile = jnp.zeros((8, 128), F32)
    row_8 = row[:, :128]
    for b in range(4):
        tile = jnp.where(row_8 == b, wave_even[:, 128 * b : 128 * b + 128], tile)
        tile = jnp.where(row_8 == 4 + b, wave_odd[:, 128 * b : 128 * b + 128], tile)
    wave_tiles[1] = tile
    near += [
        send(wave_tiles.at[1], wave_tiles.at[0], 4, (dp, right)),
        send(wave_tiles.at[1], wave_tiles.at[2], 5, (dp, left)),
    ]

    for load in (loads[1], loads[6], loads[7], loads[8]):
        load.wait()
    near[2].wait_recv()
    near[3].wait_recv()
    natural[...] = jnp.zeros(natural.shape, F32)
    for s in range(3):
        for b in range(4):
            line = target_rows[s, :, 256 * b : 256 * b + 256]
            if s == 0:
                line = jnp.where(first, 0.0, line)
            if s == 2:
                line = jnp.where(last, 0.0, line)
            natural[4 * s + b : 4 * s + b + 1, :] = line
    nh, nl = split(natural[...])
    moved = dot(jnp.concatenate([nh, nl], axis=0), table[MOVE : MOVE + 256, :])
    target_blocks[...] = jnp.zeros(target_blocks.shape, F32)
    target_blocks[0:16, :] = moved[:16] + moved[16:]
    bank, bank_fine = mels[0:512, :], mels[512:640, :]
    target_coarse = level_of(coarse_energy(coarse_spectrum(target_blocks, tapers, table)), bank)
    s = fine_spectrum(target_blocks, tapers, table)
    s = s * s
    target_fine = level_of(s[:, :128] + s[:, 128:], bank_fine)

    wave_blocks[...] = jnp.zeros(wave_blocks.shape, F32)
    near[4].wait_recv()
    near[5].wait_recv()
    for s in range(3):
        for half in range(2):
            lines = wave_tiles[s, 4 * half : 4 * half + 4, :]
            if s == 0:
                lines = jnp.where(first, 0.0, lines)
            if s == 2:
                lines = jnp.where(last, 0.0, lines)
            wave_blocks[4 * s : 4 * s + 4, 128 * half : 128 * half + 128] = lines
    parts = coarse_spectrum(wave_blocks, tapers, table)
    level = level_of(coarse_energy(parts), bank)
    frame = lax.broadcasted_iota(jnp.int32, (16, 128), 0)
    index = 4 * tm + frame - 4
    valid = (frame < 9) & (index >= 0) & (index < 4 * n_tm)
    slope = energy_slope(level, target_coarse, valid, bank)
    s0, s2, re, im = parts
    twice = functools.partial(jnp.concatenate, axis=1)
    d0 = s0 * twice([slope[:, 0:128]] * 2)
    d2 = s2 * twice([slope[:, 128:256]] * 2)
    d_even = rows_dot(d0, table[HIGH : HIGH + 256, :], table[LOW : LOW + 256, :], dot_nt)
    d_odd = rows_dot(
        d2, table[HIGH + 256 : HIGH + 512, :], table[LOW + 256 : LOW + 512, :], dot_nt
    )
    d_cross = rows_dot(
        re * slope[:, 256:512],
        table[HIGH + 512 : HIGH + 1024, :],
        table[LOW + 512 : LOW + 1024, :],
        dot_nt,
    ) + rows_dot(
        im * slope[:, 256:512],
        table[HIGH + 1024 : HIGH + 1536, :],
        table[LOW + 1024 : LOW + 1536, :],
        dot_nt,
    )
    d_first, d_second = d_cross[:, :256], d_cross[:, 256:]
    both, apart = d_even + d_odd, d_even - d_odd
    for b, d in enumerate((both + d_first, apart + d_second, both - d_first, apart - d_second)):
        frame_grads[b] = d * tapers[b : b + 1, :]
    coarse = frame_grads[0, 3:11, :]
    for b in range(1, 4):
        coarse = coarse + frame_grads[b, 3 - b : 11 - b, :]

    spectrum = fine_spectrum(wave_blocks, tapers, table)
    s = spectrum * spectrum
    level = level_of(s[:, :128] + s[:, 128:], bank_fine)
    frame = lax.broadcasted_iota(jnp.int32, (32, 128), 0)
    index = 16 * tm + 4 * (lax.rem(frame, 8) - 1) + frame // 8
    valid = (index >= 0) & (index < 16 * n_tm)
    slope = energy_slope(level, target_fine, valid, bank_fine)
    d = rows_dot(
        spectrum * twice([slope] * 2),
        table[FINE_HIGH : FINE_HIGH + 256, :],
        table[FINE_LOW : FINE_LOW + 256, :],
        dot_nt,
    )
    d = d * tapers[4:5, :]
    lane_8 = lax.broadcasted_iota(jnp.int32, (8, 128), 1)
    fine = []
    for start in (0, 128):
        here = d[0:8, start : start + 128]
        after = jnp.zeros((8, 128), F32)
        for k in range(1, 4):
            moved = roll(d[8 * k : 8 * k + 8, start : start + 128], 32 * k)
            here = here + jnp.where(lane_8 >= 32 * k, moved, 0.0)
            after = after + jnp.where(lane_8 < 32 * k, moved, 0.0)
        fine.append(here + roll(after, 1, 0))
    fine = twice(fine)
    timed = 2.0 * (wave_blocks[3:11, :] - target_blocks[3:11, :])

    row_256 = lax.broadcasted_iota(jnp.int32, (8, 256), 0)
    own = (row_256 >= 1) & (row_256 <= 4)
    lane_1 = lax.broadcasted_iota(jnp.int32, (1, 128), 1)
    line = jnp.zeros((1, 128), F32)
    for i, member in enumerate((timed, coarse, fine)):
        kept = jnp.where(own, member * member, 0.0)
        line = jnp.where(lane_1 == i, jnp.sum(kept, keepdims=True), line)
    squares[tm] = line

    def far(source, place, slot, device):
        return pltpu.make_async_remote_copy(
            src_ref=source,
            dst_ref=place,
            send_sem=far_send.at[slot],
            recv_sem=far_recv.at[slot],
            device_id=device,
            device_id_type=MESH,
        )

    def arrived(ref, slot):
        pltpu.make_async_copy(ref, ref, far_recv.at[slot]).wait()

    def sent(ref, slot):
        pltpu.make_async_copy(ref, ref, far_send.at[slot]).wait()

    @pl.loop(1, n_tm)
    def _(i):
        far(squares.at[tm], squares.at[tm], 0, (dp, lax.rem(tm + i, n_tm))).start()

    grad_blocks[0] = timed
    grad_blocks[1] = coarse
    grad_blocks[2] = fine
    arrived(squares.at[pl.ds(0, n_tm - 1)], 0)
    sums = squares[0]
    for i in range(1, n_tm):
        sums = sums + squares[i]
    scale = lax.rsqrt(sums / (n_tm * 2.0 * frames) + 1e-06)
    balanced = jnp.zeros((8, 256), F32)
    for i, coeff in enumerate(COEFFS):
        balanced = balanced + grad_blocks[i] * (coeff * scale[:, i : i + 1])
    grad_blocks[0] = balanced

    spread = []
    even_8 = lax.rem(row_8, 2) == 0
    for b in range(5):
        r = b + 1
        even = jnp.broadcast_to(grad_blocks[0, r : r + 1, 0:128], (8, 128))
        odd = jnp.broadcast_to(grad_blocks[0, r : r + 1, 128:256], (8, 128))
        lines = jnp.where(even_8, even, odd)
        if b == 4:
            even = jnp.broadcast_to(grad_blocks[0, 0:1, 0:128], (8, 128))
            odd = jnp.broadcast_to(grad_blocks[0, 0:1, 128:256], (8, 128))
            lines = jnp.where(lane_8 < 64, lines, jnp.where(even_8, even, odd))
        spread.append(lines)
    wide_grad = jnp.where(inside, jnp.concatenate(spread, axis=1), 0.0)

    def shifted(x):
        result = x
        for by, low, high in moves:
            result = jnp.where((row >= low) & (row <= high), roll(x, -by), result)
        return jnp.concatenate([result, jnp.zeros_like(result)], axis=0)

    grad_final = weight_dot(out_bwd, shifted(wide_grad))
    owned = jnp.where(lane < frames, wide_grad, 0.0)
    out_rows = gram(shifted(owned), final)[:8]
    grad_mixed = jnp.where(inside, grad_final * slope_mixed, 0.0)
    outer_rows = gram(hidden[:, :frames], grad_mixed[:, :frames])
    grad_inner = weight_dot(outer_bwd, grad_mixed) * slope_inner
    inner_rows = gram(grad_inner[:, :frames], tapped[:, :frames])
    even, odd = grad_inner[:16], grad_inner[16:]
    around = jnp.concatenate([even, odd, roll(odd, 1), roll(even, -1)], axis=0)
    grad_lifted = weight_dot(inner_bwd, around)
    grad_upper = jnp.where(inside, grad_mixed + grad_lifted * slope_upper, 0.0)
    packed[0:64, :] = gram(grad_upper[:, :frames], stacked[:, :frames])
    taps = inner_rows[:16] + roll(inner_rows[16:], -32)
    pair = outer_rows[:16, :32] + outer_rows[16:, 32:]
    packed[64:80, :] = jnp.concatenate([taps[:, :96], pair], axis=1)
    taps_7 = out_rows[0:7, 32:64] + out_rows[1:8, 0:32]
    packed[80:88, :] = jnp.zeros((8, 128), F32)
    packed[80:87, 0:32] = taps_7

    for i in range(TILES):
        owner = (i * n_plane) // TILES
        chunk = packed.at[pl.ds(8 * i, 8)]
        mine = plane == owner

        @pl.when(mine)
        def _():
            plane_rows[plane] = chunk[...]

        @pl.when(jnp.logical_not(mine))
        def _():
            far(
                chunk, plane_rows.at[plane], 1, (owner % n_dp, (owner // n_dp) * n_z + z)
            ).start()

    after = jnp.concatenate([grad_upper, roll(grad_upper, -1)], axis=0)
    grad_out[...] = weight_dot(up_bwd, after[:, :frames]) * slope_in[:, :frames]
    store = pltpu.make_async_copy(grad_out, grad_hbm.at[0], store_sem)
    store.start()

    tile_index = (plane * TILES + n_plane - 1) // n_plane
    owns = (tile_index < TILES) & ((tile_index * n_plane) // TILES == plane)
    tile_rows = pl.ds(pl.multiple_of(8 * tile_index, 8), 8)

    @pl.when(owns)
    def _():
        arrived(plane_rows.at[pl.ds(0, n_plane - 1)], 1)
        chunk = plane_rows[0]
        for i in range(1, n_plane):
            chunk = chunk + plane_rows[i]
        ring_rows[z] = chunk

        @pl.loop(1, n_z)
        def _(i):
            peer = y_hi * n_z + lax.rem(z + i, n_z)
            far(ring_rows.at[z], ring_rows.at[z], 2, (dp, peer)).start()

        arrived(ring_rows.at[pl.ds(0, n_z - 1)], 2)
        chunk = ring_rows[0]
        for i in range(1, n_z):
            chunk = chunk + ring_rows[i]
        total[tile_rows, :] = chunk

        @pl.loop(1, n_plane)
        def _(i):
            peer = lax.rem(plane + i, n_plane)
            far(
                total.at[tile_rows],
                total.at[tile_rows],
                3,
                (lax.rem(peer, n_dp), (peer // n_dp) * n_z + z),
            ).start()

        arrived(total.at[pl.ds(0, 8 * (TILES - 1))], 3)

    @pl.when(jnp.logical_not(owns))
    def _():
        arrived(total.at[pl.ds(0, 8 * TILES)], 3)

    sums = total[...]
    square = jnp.sum(sums * sums, keepdims=True)
    factor = jnp.minimum(1.0, lax.rsqrt(square / PARAMS + 1e-06))
    sums = sums * factor
    up_ref[0] = sums[0:32, 0:64]
    up_ref[1] = sums[32:64, 0:64]
    up_ref[2] = sums[0:32, 64:128]
    up_ref[3] = sums[32:64, 64:128]
    for j in range(3):
        inner_ref[j] = sums[64:80, 32 * j : 32 * j + 32]
    outer_ref[...] = sums[64:80, 96:128]
    out_ref[...] = sums[80:87, 0:32]

    for copy in near:
        copy.wait_send()
    sent(squares.at[pl.ds(0, n_tm - 1)], 0)
    store.wait()

    @pl.when(owns)
    def _():
        sent(packed.at[pl.ds(0, 8 * (TILES - 1))], 1)
        sent(ring_rows.at[pl.ds(0, n_z - 1)], 2)
        sent(plane_rows.at[pl.ds(0, n_plane - 1)], 3)

    @pl.when(jnp.logical_not(owns))
    def _():
        sent(packed.at[pl.ds(0, 8 * TILES)], 1)


def local(n_dp, n_tm, latent, target, up_kernel, inner_kernel, outer_kernel, out_kernel):
    dft, mels, tapers = tables()
    frames = latent.shape[2]
    n_z = n_tm // Y_HI
    n_plane = n_dp * Y_HI
    shape = jax.ShapeDtypeStruct
    hbm = pl.BlockSpec(memory_space=pltpu.HBM)
    vmem = pl.BlockSpec(memory_space=pltpu.VMEM)
    results = pl.pallas_call(
        functools.partial(kernel, n_dp, n_tm),
        out_shape=(
            shape(latent.shape, F32),
            shape((4, 32, 64), F32),
            shape((3, 16, 32), F32),
            shape((16, 32), F32),
            shape((7, 32), F32),
        ),
        in_specs=[hbm] * 9,
        out_specs=(hbm, vmem, vmem, vmem, vmem),
        scratch_shapes=[
            pltpu.VMEM((64, frames), F32),
            pltpu.VMEM((2, 64, 128), F32),
            pltpu.VMEM((3, 1, 2 * frames), F32),
            pltpu.VMEM((4, 32, 64), F32),
            pltpu.VMEM((3, 16, 32), F32),
            pltpu.VMEM((16, 32), F32),
            pltpu.VMEM((7, 32), F32),
            pltpu.VMEM((ROWS, 256), BF16),
            pltpu.VMEM((640, 128), BF16),
            pltpu.VMEM((8, 256), F32),
            pltpu.VMEM((16, 256), F32),
            pltpu.VMEM((24, 256), F32),
            pltpu.VMEM((3, 8, 128), F32),
            pltpu.VMEM((24, 256), F32),
            pltpu.VMEM((4, 16, 256), F32),
            pltpu.VMEM((3, 8, 256), F32),
            pltpu.VMEM((n_tm, 1, 128), F32),
            pltpu.VMEM((8 * TILES, 128), F32),
            pltpu.VMEM((n_plane, 8, 128), F32),
            pltpu.VMEM((n_z, 8, 128), F32),
            pltpu.VMEM((8 * TILES, 128), F32),
            pltpu.VMEM((64, frames), F32),
            pltpu.SemaphoreType.DMA((9,)),
            pltpu.SemaphoreType.DMA((6,)),
            pltpu.SemaphoreType.DMA((6,)),
            pltpu.SemaphoreType.DMA((4,)),
            pltpu.SemaphoreType.DMA((4,)),
            pltpu.SemaphoreType.DMA,
        ],
        compiler_params=pltpu.CompilerParams(
            collective_id=0, has_side_effects=True, vmem_limit_bytes=32 * 1024 * 1024
        ),
    )(
        latent,
        target,
        up_kernel,
        inner_kernel,
        outer_kernel.T,
        out_kernel,
        jnp.asarray(dft),
        jnp.asarray(mels),
        jnp.asarray(tapers),
    )
    grad, up, inner, outer, out = results
    return grad, up, inner, outer.T, out


def solution(mesh):
    return jax.shard_map(
        functools.partial(local, mesh.shape["dp"], mesh.shape["tm"]),
        mesh=mesh,
        in_specs=(P("dp", None, "tm"), P("dp", "tm"), P(), P(), P(), P()),
        out_specs=(P("dp", None, "tm"), P(), P(), P(), P()),
        check_vma=False,
    )
```

time: 236 us -> 70.6 us (0.30)
  the two profiles are of different devices: /device:TPU:4 before, /device:TPU:1 now
where the time goes in v1:
time: 70.6 us; the launch traced here: 70.2 us
  Pallas kernels  58.7 us (83%)
  local copies, waits for them, and re-layouts  10.8 us (15%)
    pallas_call x1, Pallas kernels, local(): pl.pallas_call(functools.partial(kernel, n_dp, n_tm), out_shape=(shape(la...  58.7 us
    unnamed x23, local copies, waits for them, and re-layouts  10.8 us

profile of v1, /device:TPU:1, one launch (start us, length us, event | category | flops | bytes accessed | tf_op | source)
XLA Modules:
  0.0 70.2 jit_solution(5339493670429577163)
XLA Ops:
  0.6 0.0 copy-start
  0.6 1.5 %copy-done = bf16[3840,256]{1,0:T(8,128)(2,1)S(1)} copy-done((bf16[3840,256]{1,0:T(8,128)(2,1)S(1)}, bf16[3840,256]{1,0:T(8,128)(2,1)}, u32[]{:S(2)}) %copy-start) | copy-done | bytes 1966104
  2.2 0.0 copy-start.1
  2.2 0.9 %copy-done.1 = bf16[640,128]{1,0:T(8,128)(2,1)S(1)} copy-done((bf16[640,128]{1,0:T(8,128)(2,1)S(1)}, bf16[640,128]{1,0:T(8,128)(2,1)}, u32[]{:S(2)}) %copy-start.1) | copy-done | bytes 163864
  3.1 0.0 copy-start.2
  3.1 0.9 %copy-done.2 = f32[1,64,512]{2,1,0:T(8,128)S(1)} copy-done((f32[1,64,512]{2,1,0:T(8,128)S(1)}, f32[1,64,512]{2,1,0:T(8,128)}, u32[]{:S(2)}) %copy-start.2) | copy-done | bytes 131096
  4.0 0.0 copy-start.3
  4.0 0.8 %copy-done.3 = f32[4,32,64]{2,1,0:T(8,128)S(1)} copy-done((f32[4,32,64]{2,1,0:T(8,128)S(1)}, f32[4,32,64]{2,1,0:T(8,128)}, u32[]{:S(2)}) %copy-start.3) | copy-done | bytes 32792
  4.8 0.0 copy-start.4
  4.8 0.7 %copy-done.4 = f32[3,16,32]{2,1,0:T(8,128)S(1)} copy-done((f32[3,16,32]{2,1,0:T(8,128)S(1)}, f32[3,16,32]{2,1,0:T(8,128)}, u32[]{:S(2)}) %copy-start.4) | copy-done | bytes 6168
  5.6 0.0 copy-start.5
  5.6 0.7 copy-done.5
  6.3 0.0 copy-start.6
  6.3 0.7 copy-done.6
  7.0 0.0 copy-start.7
  7.0 0.7 copy-done.7
  7.7 0.0 copy-start.8
  7.7 0.7 copy-done.8
  8.4 58.7 %shard_map.128 = (f32[1,64,512]{2,1,0:T(8,128)S(1)}, f32[4,32,64]{2,1,0:T(8,128)S(1)}, f32[3,16,32]{2,1,0:T(8,128)S(1)}, f32[16,32]{1,0:T(8,128)S(1)}, f32[7,32]{1,0:T(8,128)S(1)}) custom-call(f32[1,64,512]{2,1,0:T(8,128)S(1)} %copy-done.2, f32[1,1024]{1,0:T(1,128)S(1)} %copy-done.7, f32[4,32,64]{2,1,0:T(8,128)S(1)} %copy-done.3, ...), custom_call_target="tpu_custom_call" | custom-call | tf_op jit(solution)/shard_map/pallas_call | solution.py:679
  67.1 0.7 copy.19
  67.7 0.6 copy.20
  68.4 0.6 copy.21
  69.0 0.6 copy.22
  69.6 0.6 copy.23
Async XLA Ops:
  0.6 1.5 %copy-start = (bf16[3840,256]{1,0:T(8,128)(2,1)S(1)}, bf16[3840,256]{1,0:T(8,128)(2,1)}, u32[]{:S(2)}) copy-start(bf16[3840,256]{1,0:T(8,128)(2,1)} %constant.6.clone.dft_hbm) | copy-start | bytes 5898244
  2.2 0.9 %copy-start.1 = (bf16[640,128]{1,0:T(8,128)(2,1)S(1)}, bf16[640,128]{1,0:T(8,128)(2,1)}, u32[]{:S(2)}) copy-start(bf16[640,128]{1,0:T(8,128)(2,1)} %constant.7.clone.mels_hbm) | copy-start | bytes 491524
  3.1 0.9 %copy-start.2 = (f32[1,64,512]{2,1,0:T(8,128)S(1)}, f32[1,64,512]{2,1,0:T(8,128)}, u32[]{:S(2)}) copy-start(f32[1,64,512]{2,1,0:T(8,128)} %latent_hbm.1) | copy-start | bytes 393220
  4.0 0.8 %copy-start.3 = (f32[4,32,64]{2,1,0:T(8,128)S(1)}, f32[4,32,64]{2,1,0:T(8,128)}, u32[]{:S(2)}) copy-start(f32[4,32,64]{2,1,0:T(8,128)} %up_hbm.1) | copy-start | bytes 98308
  4.8 0.7 %copy-start.4 = (f32[3,16,32]{2,1,0:T(8,128)S(1)}, f32[3,16,32]{2,1,0:T(8,128)}, u32[]{:S(2)}) copy-start(f32[3,16,32]{2,1,0:T(8,128)} %inner_hbm.1) | copy-start | bytes 18436
  5.6 0.7 copy-start.5
  6.3 0.7 copy-start.6
  7.0 0.7 copy-start.7
  7.7 0.7 copy-start.8

commit v2 on v1

--- a/solution.py
+++ b/solution.py
@@ -200,11 +200,8 @@
     dft_hbm,
     mels_hbm,
     tapers_hbm,
-    grad_hbm,
-    up_ref,
-    inner_ref,
-    outer_ref,
-    out_ref,
+    grad_out,
+    total,
     latent,
     halo,
     target_rows,
@@ -225,14 +222,11 @@
     packed,
     plane_rows,
     ring_rows,
-    total,
-    grad_out,
     load_sem,
     near_send,
     near_recv,
     far_send,
     far_recv,
-    store_sem,
 ):
     dp = lax.axis_index("dp")
     tm = lax.axis_index("tm")
@@ -597,8 +591,6 @@
 
     after = jnp.concatenate([grad_upper, roll(grad_upper, -1)], axis=0)
     grad_out[...] = weight_dot(up_bwd, after[:, :frames]) * slope_in[:, :frames]
-    store = pltpu.make_async_copy(grad_out, grad_hbm.at[0], store_sem)
-    store.start()
 
     tile_index = (plane * TILES + n_plane - 1) // n_plane
     owns = (tile_index < TILES) & ((tile_index * n_plane) // TILES == plane)
@@ -639,7 +631,24 @@
     def _():
         arrived(total.at[pl.ds(0, 8 * TILES)], 3)
 
-    sums = total[...]
+    for copy in near:
+        copy.wait_send()
+    sent(squares.at[pl.ds(0, n_tm - 1)], 0)
+
+    @pl.when(owns)
+    def _():
+        sent(packed.at[pl.ds(0, 8 * (TILES - 1))], 1)
+        sent(ring_rows.at[pl.ds(0, n_z - 1)], 2)
+        sent(plane_rows.at[pl.ds(0, n_plane - 1)], 3)
+
+    @pl.when(jnp.logical_not(owns))
+    def _():
+        sent(packed.at[pl.ds(0, 8 * TILES)], 1)
+
+
+def finish(grad_ref, total_ref, latent_ref, up_ref, inner_ref, outer_ref, out_ref):
+    latent_ref[0] = grad_ref[...]
+    sums = total_ref[...]
     square = jnp.sum(sums * sums, keepdims=True)
     factor = jnp.minimum(1.0, lax.rsqrt(square / PARAMS + 1e-06))
     sums = sums * factor
@@ -652,21 +661,6 @@
     outer_ref[...] = sums[64:80, 96:128]
     out_ref[...] = sums[80:87, 0:32]
 
-    for copy in near:
-        copy.wait_send()
-    sent(squares.at[pl.ds(0, n_tm - 1)], 0)
-    store.wait()
-
-    @pl.when(owns)
-    def _():
-        sent(packed.at[pl.ds(0, 8 * (TILES - 1))], 1)
-        sent(ring_rows.at[pl.ds(0, n_z - 1)], 2)
-        sent(plane_rows.at[pl.ds(0, n_plane - 1)], 3)
-
-    @pl.when(jnp.logical_not(owns))
-    def _():
-        sent(packed.at[pl.ds(0, 8 * TILES)], 1)
-
 
 def local(n_dp, n_tm, latent, target, up_kernel, inner_kernel, outer_kernel, out_kernel):
     dft, mels, tapers = tables()
@@ -676,17 +670,11 @@
     shape = jax.ShapeDtypeStruct
     hbm = pl.BlockSpec(memory_space=pltpu.HBM)
     vmem = pl.BlockSpec(memory_space=pltpu.VMEM)
-    results = pl.pallas_call(
+    grad, total = pl.pallas_call(
         functools.partial(kernel, n_dp, n_tm),
-        out_shape=(
-            shape(latent.shape, F32),
-            shape((4, 32, 64), F32),
-            shape((3, 16, 32), F32),
-            shape((16, 32), F32),
-            shape((7, 32), F32),
-        ),
+        out_shape=(shape((64, frames), F32), shape((8 * TILES, 128), F32)),
         in_specs=[hbm] * 9,
-        out_specs=(hbm, vmem, vmem, vmem, vmem),
+        out_specs=(vmem, vmem),
         scratch_shapes=[
             pltpu.VMEM((64, frames), F32),
             pltpu.VMEM((2, 64, 128), F32),
@@ -708,17 +696,14 @@
             pltpu.VMEM((8 * TILES, 128), F32),
             pltpu.VMEM((n_plane, 8, 128), F32),
             pltpu.VMEM((n_z, 8, 128), F32),
-            pltpu.VMEM((8 * TILES, 128), F32),
-            pltpu.VMEM((64, frames), F32),
             pltpu.SemaphoreType.DMA((9,)),
             pltpu.SemaphoreType.DMA((6,)),
             pltpu.SemaphoreType.DMA((6,)),
             pltpu.SemaphoreType.DMA((4,)),
             pltpu.SemaphoreType.DMA((4,)),
-            pltpu.SemaphoreType.DMA,
         ],
         compiler_params=pltpu.CompilerParams(
-            collective_id=0, has_side_effects=True, vmem_limit_bytes=32 * 1024 * 1024
+            collective_id=0, has_side_effects=True, vmem_limit_bytes=60 * 1024 * 1024
         ),
     )(
         latent,
@@ -731,7 +716,18 @@
         jnp.asarray(mels),
         jnp.asarray(tapers),
     )
-    grad, up, inner, outer, out = results
+    grad, up, inner, outer, out = pl.pallas_call(
+        finish,
+        out_shape=(
+            shape(latent.shape, F32),
+            shape((4, 32, 64), F32),
+            shape((3, 16, 32), F32),
+            shape((16, 32), F32),
+            shape((7, 32), F32),
+        ),
+        in_specs=[vmem] * 2,
+        out_specs=(vmem,) * 5,
+    )(grad, total)
     return grad, up, inner, outer.T, out
 
 

time: 70.6 us -> 61.9 us (0.88)
  local copies, waits for them, and re-layouts: 10.8 us -> 0 us
  Pallas kernels: 58.7 us -> 61.1 us
    unnamed x23 -> x0, local copies, waits for them, and re-layouts: 10.8 us -> none
    pallas_call x1 -> x2, Pallas kernels: 58.7 us -> 61.1 us  [the longest x1 59.4 us: local(): pl.pallas_call(functools.partial(kernel, n_dp, n_tm), out_shape=(shape((6...]
where the time goes in v2:
time: 61.9 us; the launch traced here: 61.8 us
  Pallas kernels  61.1 us (99%)
  between operations  0.64 us (1%)
    pallas_call x1, Pallas kernels, local(): pl.pallas_call(functools.partial(kernel, n_dp, n_tm), out_shape=(shape((6...  59.4 us
    pallas_call x1, Pallas kernels, local(): pl.pallas_call(finish, out_shape=(shape(latent.shape, F32), shape((4, 32,...  1.77 us

profile of v2, /device:TPU:1, one launch (start us, length us, event | category | flops | bytes accessed | tf_op | source)
XLA Modules:
  0.0 61.8 jit_solution(13536021286601187003)
XLA Ops:
  0.6 59.4 %shard_map.128 = (f32[64,512]{1,0:T(8,128)}, f32[88,128]{1,0:T(8,128)}) custom-call(f32[1,64,512]{2,1,0:T(8,128)} %latent_hbm.1, f32[1,1024]{1,0:T(1,128)} %target_hbm.1, f32[4,32,64]{2,1,0:T(8,128)} %up_hbm.1, f32[3,16,32]{2,1,0:T(8,128)} %inner_hbm.1, f32[16,32]{1,0:T(8,128)} %bitcast.2, f32[7,32]{1,0:T(8,128)} %out_hbm.1, ...), custom_call_target="tpu_custom_call" | custom-call | tf_op jit(solution)/shard_map/pallas_call | solution.py:673
  60.0 1.8 %shard_map.129 = (f32[1,64,512]{2,1,0:T(8,128)}, f32[4,32,64]{2,1,0:T(8,128)}, f32[3,16,32]{2,1,0:T(8,128)}, f32[16,32]{1,0:T(8,128)}, f32[7,32]{1,0:T(8,128)}) custom-call(f32[64,512]{1,0:T(8,128)} %get-tuple-element.12.grad_ref, f32[88,128]{1,0:T(8,128)} %get-tuple-element.13.total_ref), custom_call_target="tpu_custom_call" | custom-call | tf_op jit(solution)/shard_map/pallas_call | solution.py:719

commit v3 on v2

--- a/solution.py
+++ b/solution.py
@@ -220,6 +220,8 @@
     grad_blocks,
     squares,
     packed,
+    packed_rows,
+    grad_rows,
     plane_rows,
     ring_rows,
     load_sem,
@@ -243,18 +245,55 @@
 
     barrier = pltpu.get_barrier_semaphore()
 
+    def owner_of(index):
+        return (index * n_plane) // TILES
+
+    def tile_of(member):
+        return (member * TILES + n_plane - 1) // n_plane
+
+    def is_owner(member):
+        index = tile_of(member)
+        return (index < TILES) & (owner_of(index) == member)
+
+    def along_z(i):
+        half = (i + 1) // 2
+        return lax.rem(z + n_z // 2 + half - 2 * half * lax.rem(i, 2) + n_z, n_z)
+
+    def in_plane(visit):
+        core, x, y_lo = lax.rem(dp, 2), lax.rem(dp // 2, 4), dp // 8
+        for dx in (2, 1, 3, 0):
+
+            @pl.loop(0, 8 if dx else 7)
+            def _(i):
+                bits = 7 - i
+                y = lax.rem(y_hi + bits // 4, 2)
+                y_in = lax.rem(y_lo + lax.rem(bits // 2, 2), 2)
+                side = lax.rem(core + lax.rem(bits, 2), 2)
+                visit(y * n_dp + y_in * 8 + lax.rem(x + dx, 4) * 2 + side)
+
+    def member_id(member):
+        return (lax.rem(member, n_dp), (member // n_dp) * n_z + z)
+
+    owns = is_owner(plane)
+    partner = lax.rem(y_hi + 1, Y_HI) * n_dp + dp
+
     def greet(device):
         pl.semaphore_signal(barrier, inc=1, device_id=device, device_id_type=MESH)
 
-    @pl.loop(1, n_tm)
+    @pl.loop(0, n_z - 1)
     def _(i):
-        greet((dp, lax.rem(tm + i, n_tm)))
-
-    @pl.loop(1, n_dp)
-    def _(i):
-        peer = lax.rem(dp + i, n_dp)
-        greet((peer, tm))
-        greet((peer, other))
+        greet((dp, y_hi * n_z + along_z(i)))
+        greet((dp, other - z + along_z(i)))
+
+    greet((dp, other))
+
+    def greet_member(member):
+        @pl.when((owns | is_owner(member)) & (member != partner))
+        def _():
+            greet(member_id(member))
+
+    in_plane(greet_member)
+    greeted = jnp.where(owns, n_plane - 2, TILES - jnp.where(is_owner(partner), 1, 0))
 
     loads = [
         pltpu.make_async_copy(source, place, load_sem.at[i])
@@ -329,7 +368,17 @@
     out_fwd = split(out_w16)
     out_bwd = split(out_w16.T)
 
-    pl.semaphore_wait(barrier, n_tm - 1 + 2 * (n_dp - 1))
+    loads[0].wait()
+    lane_8 = lax.broadcasted_iota(jnp.int32, (8, 128), 1)
+    lent = jnp.zeros((8, 128), F32)
+    for g in range(8):
+        start = latent[8 * g : 8 * g + 8, 0:128]
+        end = latent[8 * g : 8 * g + 8, frames - 128 : frames]
+        lent = jnp.where(lane_8 // 4 == g, roll(start, 4 * g), lent)
+        lent = jnp.where(lane_8 // 4 == 16 + g, roll(end, 4 * g - 60), lent)
+    halo[1] = lent
+
+    pl.semaphore_wait(barrier, n_tm - 1 + greeted)
 
     def send(source, place, slot, device):
         copy = pltpu.make_async_remote_copy(
@@ -344,8 +393,8 @@
         return copy
 
     near = [
-        send(latent_hbm.at[0, :, pl.ds(frames - 128, 128)], halo.at[0], 0, (dp, right)),
-        send(latent_hbm.at[0, :, pl.ds(0, 128)], halo.at[1], 1, (dp, left)),
+        send(halo.at[1], halo.at[0], 0, (dp, right)),
+        send(halo.at[1], halo.at[2], 1, (dp, left)),
         send(target_hbm, target_rows.at[0], 2, (dp, right)),
         send(target_hbm, target_rows.at[2], 3, (dp, left)),
     ]
@@ -357,15 +406,16 @@
         | ((lane >= wide - 4) & jnp.logical_not(first))
     )
 
-    loads[0].wait()
     near[0].wait_recv()
     near[1].wait_recv()
-    spot = lax.broadcasted_iota(jnp.int32, (64, 128), 1)
-    rim = jnp.where(
-        (spot < 4) & jnp.logical_not(last),
-        halo[1],
-        jnp.where((spot >= 124) & jnp.logical_not(first), halo[0], 0.0),
-    )
+    before, behind = halo[0], halo[2]
+    rim = []
+    for g in range(8):
+        tile = jnp.where((lane_8 < 4) & jnp.logical_not(last), roll(behind, -4 * g), 0.0)
+        rim.append(
+            jnp.where((lane_8 >= 124) & jnp.logical_not(first), roll(before, 60 - 4 * g), tile)
+        )
+    rim = jnp.concatenate(rim, axis=0)
     activated, slope_in = elu_and_slope(jnp.concatenate([latent[...], rim], axis=1))
     stacked = jnp.concatenate([activated, roll(activated, 1)], axis=0)
     upper = jnp.where(inside, weight_dot(up_fwd, stacked), 0.0)
@@ -480,7 +530,6 @@
         dot_nt,
     )
     d = d * tapers[4:5, :]
-    lane_8 = lax.broadcasted_iota(jnp.int32, (8, 128), 1)
     fine = []
     for start in (0, 128):
         here = d[0:8, start : start + 128]
@@ -518,64 +567,72 @@
     def sent(ref, slot):
         pltpu.make_async_copy(ref, ref, far_send.at[slot]).wait()
 
-    @pl.loop(1, n_tm)
+    @pl.loop(0, n_z - 1)
     def _(i):
-        far(squares.at[tm], squares.at[tm], 0, (dp, lax.rem(tm + i, n_tm))).start()
+        far(squares.at[tm], squares.at[tm], 0, (dp, other - z + along_z(i))).start()
+        far(squares.at[tm], squares.at[tm], 0, (dp, y_hi * n_z + along_z(i))).start()
+
+    far(squares.at[tm], squares.at[tm], 0, (dp, other)).start()
 
     grad_blocks[0] = timed
     grad_blocks[1] = coarse
     grad_blocks[2] = fine
+    even_8 = lax.rem(row_8, 2) == 0
+
+    def shifted(x):
+        result = x
+        for by, low, high in moves:
+            result = jnp.where((row >= low) & (row <= high), roll(x, -by), result)
+        return jnp.concatenate([result, jnp.zeros_like(result)], axis=0)
+
+    for i in range(3):
+        spread = []
+        for b in range(5):
+            r = b + 1
+            even = jnp.broadcast_to(grad_blocks[i, r : r + 1, 0:128], (8, 128))
+            odd = jnp.broadcast_to(grad_blocks[i, r : r + 1, 128:256], (8, 128))
+            lines = jnp.where(even_8, even, odd)
+            if b == 4:
+                even = jnp.broadcast_to(grad_blocks[i, 0:1, 0:128], (8, 128))
+                odd = jnp.broadcast_to(grad_blocks[i, 0:1, 128:256], (8, 128))
+                lines = jnp.where(lane_8 < 64, lines, jnp.where(even_8, even, odd))
+            spread.append(lines)
+        wide_grad = jnp.where(inside, jnp.concatenate(spread, axis=1), 0.0)
+        grad_final = weight_dot(out_bwd, shifted(wide_grad))
+        owned = jnp.where(lane < frames, wide_grad, 0.0)
+        out_rows = gram(shifted(owned), final)[:8]
+        grad_mixed = jnp.where(inside, grad_final * slope_mixed, 0.0)
+        outer_rows = gram(hidden[:, :frames], grad_mixed[:, :frames])
+        grad_inner = weight_dot(outer_bwd, grad_mixed) * slope_inner
+        inner_rows = gram(grad_inner[:, :frames], tapped[:, :frames])
+        even, odd = grad_inner[:16], grad_inner[16:]
+        around = jnp.concatenate([even, odd, roll(odd, 1), roll(even, -1)], axis=0)
+        grad_lifted = weight_dot(inner_bwd, around)
+        grad_upper = jnp.where(inside, grad_mixed + grad_lifted * slope_upper, 0.0)
+        packed_rows[i, 0:64, :] = gram(grad_upper[:, :frames], stacked[:, :frames])
+        taps = inner_rows[:16] + roll(inner_rows[16:], -32)
+        pair = outer_rows[:16, :32] + outer_rows[16:, 32:]
+        packed_rows[i, 64:80, :] = jnp.concatenate([taps[:, :96], pair], axis=1)
+        taps_7 = out_rows[0:7, 32:64] + out_rows[1:8, 0:32]
+        packed_rows[i, 80:88, :] = jnp.zeros((8, 128), F32)
+        packed_rows[i, 80:87, 0:32] = taps_7
+        after = jnp.concatenate([grad_upper, roll(grad_upper, -1)], axis=0)
+        grad_rows[i] = weight_dot(up_bwd, after[:, :frames]) * slope_in[:, :frames]
+
     arrived(squares.at[pl.ds(0, n_tm - 1)], 0)
     sums = squares[0]
     for i in range(1, n_tm):
         sums = sums + squares[i]
     scale = lax.rsqrt(sums / (n_tm * 2.0 * frames) + 1e-06)
-    balanced = jnp.zeros((8, 256), F32)
-    for i, coeff in enumerate(COEFFS):
-        balanced = balanced + grad_blocks[i] * (coeff * scale[:, i : i + 1])
-    grad_blocks[0] = balanced
-
-    spread = []
-    even_8 = lax.rem(row_8, 2) == 0
-    for b in range(5):
-        r = b + 1
-        even = jnp.broadcast_to(grad_blocks[0, r : r + 1, 0:128], (8, 128))
-        odd = jnp.broadcast_to(grad_blocks[0, r : r + 1, 128:256], (8, 128))
-        lines = jnp.where(even_8, even, odd)
-        if b == 4:
-            even = jnp.broadcast_to(grad_blocks[0, 0:1, 0:128], (8, 128))
-            odd = jnp.broadcast_to(grad_blocks[0, 0:1, 128:256], (8, 128))
-            lines = jnp.where(lane_8 < 64, lines, jnp.where(even_8, even, odd))
-        spread.append(lines)
-    wide_grad = jnp.where(inside, jnp.concatenate(spread, axis=1), 0.0)
-
-    def shifted(x):
-        result = x
-        for by, low, high in moves:
-            result = jnp.where((row >= low) & (row <= high), roll(x, -by), result)
-        return jnp.concatenate([result, jnp.zeros_like(result)], axis=0)
-
-    grad_final = weight_dot(out_bwd, shifted(wide_grad))
-    owned = jnp.where(lane < frames, wide_grad, 0.0)
-    out_rows = gram(shifted(owned), final)[:8]
-    grad_mixed = jnp.where(inside, grad_final * slope_mixed, 0.0)
-    outer_rows = gram(hidden[:, :frames], grad_mixed[:, :frames])
-    grad_inner = weight_dot(outer_bwd, grad_mixed) * slope_inner
-    inner_rows = gram(grad_inner[:, :frames], tapped[:, :frames])
-    even, odd = grad_inner[:16], grad_inner[16:]
-    around = jnp.concatenate([even, odd, roll(odd, 1), roll(even, -1)], axis=0)
-    grad_lifted = weight_dot(inner_bwd, around)
-    grad_upper = jnp.where(inside, grad_mixed + grad_lifted * slope_upper, 0.0)
-    packed[0:64, :] = gram(grad_upper[:, :frames], stacked[:, :frames])
-    taps = inner_rows[:16] + roll(inner_rows[16:], -32)
-    pair = outer_rows[:16, :32] + outer_rows[16:, 32:]
-    packed[64:80, :] = jnp.concatenate([taps[:, :96], pair], axis=1)
-    taps_7 = out_rows[0:7, 32:64] + out_rows[1:8, 0:32]
-    packed[80:88, :] = jnp.zeros((8, 128), F32)
-    packed[80:87, 0:32] = taps_7
+    scales = [coeff * scale[:, i : i + 1] for i, coeff in enumerate(COEFFS)]
+
+    def combined(rows):
+        return scales[0] * rows[0] + scales[1] * rows[1] + scales[2] * rows[2]
+
+    packed[...] = combined(packed_rows)
 
     for i in range(TILES):
-        owner = (i * n_plane) // TILES
+        owner = owner_of(i)
         chunk = packed.at[pl.ds(8 * i, 8)]
         mine = plane == owner
 
@@ -589,11 +646,9 @@
                 chunk, plane_rows.at[plane], 1, (owner % n_dp, (owner // n_dp) * n_z + z)
             ).start()
 
-    after = jnp.concatenate([grad_upper, roll(grad_upper, -1)], axis=0)
-    grad_out[...] = weight_dot(up_bwd, after[:, :frames]) * slope_in[:, :frames]
-
-    tile_index = (plane * TILES + n_plane - 1) // n_plane
-    owns = (tile_index < TILES) & ((tile_index * n_plane) // TILES == plane)
+    grad_out[...] = combined(grad_rows)
+
+    tile_index = tile_of(plane)
     tile_rows = pl.ds(pl.multiple_of(8 * tile_index, 8), 8)
 
     @pl.when(owns)
@@ -604,10 +659,9 @@
             chunk = chunk + plane_rows[i]
         ring_rows[z] = chunk
 
-        @pl.loop(1, n_z)
+        @pl.loop(0, n_z - 1)
         def _(i):
-            peer = y_hi * n_z + lax.rem(z + i, n_z)
-            far(ring_rows.at[z], ring_rows.at[z], 2, (dp, peer)).start()
+            far(ring_rows.at[z], ring_rows.at[z], 2, (dp, y_hi * n_z + along_z(i))).start()
 
         arrived(ring_rows.at[pl.ds(0, n_z - 1)], 2)
         chunk = ring_rows[0]
@@ -615,16 +669,10 @@
             chunk = chunk + ring_rows[i]
         total[tile_rows, :] = chunk
 
-        @pl.loop(1, n_plane)
-        def _(i):
-            peer = lax.rem(plane + i, n_plane)
-            far(
-                total.at[tile_rows],
-                total.at[tile_rows],
-                3,
-                (lax.rem(peer, n_dp), (peer // n_dp) * n_z + z),
-            ).start()
-
+        def give(member):
+            far(total.at[tile_rows], total.at[tile_rows], 3, member_id(member)).start()
+
+        in_plane(give)
         arrived(total.at[pl.ds(0, 8 * (TILES - 1))], 3)
 
     @pl.when(jnp.logical_not(owns))
@@ -677,7 +725,7 @@
         out_specs=(vmem, vmem),
         scratch_shapes=[
             pltpu.VMEM((64, frames), F32),
-            pltpu.VMEM((2, 64, 128), F32),
+            pltpu.VMEM((3, 8, 128), F32),
             pltpu.VMEM((3, 1, 2 * frames), F32),
             pltpu.VMEM((4, 32, 64), F32),
             pltpu.VMEM((3, 16, 32), F32),
@@ -694,6 +742,8 @@
             pltpu.VMEM((3, 8, 256), F32),
             pltpu.VMEM((n_tm, 1, 128), F32),
             pltpu.VMEM((8 * TILES, 128), F32),
+            pltpu.VMEM((3, 8 * TILES, 128), F32),
+            pltpu.VMEM((3, 64, frames), F32),
             pltpu.VMEM((n_plane, 8, 128), F32),
             pltpu.VMEM((n_z, 8, 128), F32),
             pltpu.SemaphoreType.DMA((9,)),

time: 61.9 us -> 58.2 us (0.940)
  Pallas kernels: 61.1 us -> 57.4 us
    pallas_call x1, Pallas kernels: 59.4 us -> 55.6 us  [local(): pl.pallas_call(functools.partial(kernel, n_dp, n_tm), out_shape=(shape((6...]
where the time goes in v3:
time: 58.2 us; the launch traced here: 58 us
  Pallas kernels  57.4 us (99%)
  between operations  0.64 us (1%)
    pallas_call x1, Pallas kernels, local(): pl.pallas_call(functools.partial(kernel, n_dp, n_tm), out_shape=(shape((6...  55.6 us
    pallas_call x1, Pallas kernels, local(): pl.pallas_call(finish, out_shape=(shape(latent.shape, F32), shape((4, 32,...  1.77 us

profile of v3, /device:TPU:1, one launch (start us, length us, event | category | flops | bytes accessed | tf_op | source)
XLA Modules:
  0.0 58.0 jit_solution(13300238494606418045)
XLA Ops:
  0.6 55.6 %shard_map.128 = (f32[64,512]{1,0:T(8,128)}, f32[88,128]{1,0:T(8,128)}) custom-call(f32[1,64,512]{2,1,0:T(8,128)} %latent_hbm.1, f32[1,1024]{1,0:T(1,128)} %target_hbm.1, f32[4,32,64]{2,1,0:T(8,128)} %up_hbm.1, f32[3,16,32]{2,1,0:T(8,128)} %inner_hbm.1, f32[16,32]{1,0:T(8,128)} %bitcast.2, f32[7,32]{1,0:T(8,128)} %out_hbm.1, ...), custom_call_target="tpu_custom_call" | custom-call | tf_op jit(solution)/shard_map/pallas_call | solution.py:721
  56.2 1.8 %shard_map.129 = (f32[1,64,512]{2,1,0:T(8,128)}, f32[4,32,64]{2,1,0:T(8,128)}, f32[3,16,32]{2,1,0:T(8,128)}, f32[16,32]{1,0:T(8,128)}, f32[7,32]{1,0:T(8,128)}) custom-call(f32[64,512]{1,0:T(8,128)} %get-tuple-element.12.grad_ref, f32[88,128]{1,0:T(8,128)} %get-tuple-element.13.total_ref), custom_call_target="tpu_custom_call" | custom-call | tf_op jit(solution)/shard_map/pallas_call | solution.py:769

commit v4 on v3

--- a/solution.py
+++ b/solution.py
@@ -219,9 +219,10 @@
     frame_grads,
     grad_blocks,
     squares,
-    packed,
     packed_rows,
     grad_rows,
+    halves_own,
+    plane_halves,
     plane_rows,
     ring_rows,
     load_sem,
@@ -283,9 +284,16 @@
     @pl.loop(0, n_z - 1)
     def _(i):
         greet((dp, y_hi * n_z + along_z(i)))
-        greet((dp, other - z + along_z(i)))
 
     greet((dp, other))
+
+    @pl.when(z == n_z - 1)
+    def _():
+        greet((dp, right))
+
+    @pl.when(z == 0)
+    def _():
+        greet((dp, left))
 
     def greet_member(member):
         @pl.when((owns | is_owner(member)) & (member != partner))
@@ -293,7 +301,8 @@
             greet(member_id(member))
 
     in_plane(greet_member)
-    greeted = jnp.where(owns, n_plane - 2, TILES - jnp.where(is_owner(partner), 1, 0))
+    greeted = n_z + jnp.where((z == 0) | (z == n_z - 1), 1, 0)
+    greeted += jnp.where(owns, n_plane - 2, TILES - jnp.where(is_owner(partner), 1, 0))
 
     loads = [
         pltpu.make_async_copy(source, place, load_sem.at[i])
@@ -378,7 +387,7 @@
         lent = jnp.where(lane_8 // 4 == 16 + g, roll(end, 4 * g - 60), lent)
     halo[1] = lent
 
-    pl.semaphore_wait(barrier, n_tm - 1 + greeted)
+    pl.semaphore_wait(barrier, greeted)
 
     def send(source, place, slot, device):
         copy = pltpu.make_async_remote_copy(
@@ -549,7 +558,7 @@
     for i, member in enumerate((timed, coarse, fine)):
         kept = jnp.where(own, member * member, 0.0)
         line = jnp.where(lane_1 == i, jnp.sum(kept, keepdims=True), line)
-    squares[tm] = line
+    squares[z] = line
 
     def far(source, place, slot, device):
         return pltpu.make_async_remote_copy(
@@ -569,10 +578,7 @@
 
     @pl.loop(0, n_z - 1)
     def _(i):
-        far(squares.at[tm], squares.at[tm], 0, (dp, other - z + along_z(i))).start()
-        far(squares.at[tm], squares.at[tm], 0, (dp, y_hi * n_z + along_z(i))).start()
-
-    far(squares.at[tm], squares.at[tm], 0, (dp, other)).start()
+        far(squares.at[z], squares.at[z], 0, (dp, y_hi * n_z + along_z(i))).start()
 
     grad_blocks[0] = timed
     grad_blocks[1] = coarse
@@ -619,21 +625,9 @@
         after = jnp.concatenate([grad_upper, roll(grad_upper, -1)], axis=0)
         grad_rows[i] = weight_dot(up_bwd, after[:, :frames]) * slope_in[:, :frames]
 
-    arrived(squares.at[pl.ds(0, n_tm - 1)], 0)
-    sums = squares[0]
-    for i in range(1, n_tm):
-        sums = sums + squares[i]
-    scale = lax.rsqrt(sums / (n_tm * 2.0 * frames) + 1e-06)
-    scales = [coeff * scale[:, i : i + 1] for i, coeff in enumerate(COEFFS)]
-
-    def combined(rows):
-        return scales[0] * rows[0] + scales[1] * rows[1] + scales[2] * rows[2]
-
-    packed[...] = combined(packed_rows)
-
     for i in range(TILES):
         owner = owner_of(i)
-        chunk = packed.at[pl.ds(8 * i, 8)]
+        chunk = packed_rows.at[:, pl.ds(8 * i, 8)]
         mine = plane == owner
 
         @pl.when(mine)
@@ -642,11 +636,36 @@
 
         @pl.when(jnp.logical_not(mine))
         def _():
-            far(
-                chunk, plane_rows.at[plane], 1, (owner % n_dp, (owner // n_dp) * n_z + z)
-            ).start()
-
-    grad_out[...] = combined(grad_rows)
+            far(chunk, plane_rows.at[plane], 1, member_id(owner)).start()
+
+    arrived(squares.at[pl.ds(0, n_z - 1)], 0)
+    sums = squares[0]
+    for i in range(1, n_z):
+        sums = sums + squares[i]
+    halves_own[0] = sums
+    for i in range(TILES):
+        owner = owner_of(i)
+        mine = plane == owner
+
+        @pl.when(mine)
+        def _():
+            plane_halves[plane] = sums
+
+        @pl.when(jnp.logical_not(mine))
+        def _():
+            far(halves_own.at[0], plane_halves.at[plane], 4, member_id(owner)).start()
+
+    far(halves_own.at[0], halves_own.at[1], 5, (dp, other)).start()
+
+    def scales_of(sums):
+        coeffs = jnp.where(lane_1 == 0, COEFFS[0], jnp.where(lane_1 == 1, COEFFS[1], COEFFS[2]))
+        return coeffs * lax.rsqrt(sums / (n_tm * 2.0 * frames) + 1e-06)
+
+    arrived(halves_own.at[1], 5)
+    scales = scales_of(halves_own[0] + halves_own[1])
+    grad_out[...] = (
+        scales[:, 0:1] * grad_rows[0] + scales[:, 1:2] * grad_rows[1] + scales[:, 2:3] * grad_rows[2]
+    )
 
     tile_index = tile_of(plane)
     tile_rows = pl.ds(pl.multiple_of(8 * tile_index, 8), 8)
@@ -654,9 +673,13 @@
     @pl.when(owns)
     def _():
         arrived(plane_rows.at[pl.ds(0, n_plane - 1)], 1)
-        chunk = plane_rows[0]
-        for i in range(1, n_plane):
-            chunk = chunk + plane_rows[i]
+        arrived(plane_halves.at[pl.ds(0, n_plane - 1)], 4)
+        chunk = jnp.zeros((8, 128), F32)
+        for c in range(n_dp):
+            scales = scales_of(plane_halves[c] + plane_halves[n_dp + c])
+            for i in range(3):
+                both = plane_rows[c, i] + plane_rows[n_dp + c, i]
+                chunk = chunk + scales[:, i : i + 1] * both
         ring_rows[z] = chunk
 
         @pl.loop(0, n_z - 1)
@@ -681,21 +704,25 @@
 
     for copy in near:
         copy.wait_send()
-    sent(squares.at[pl.ds(0, n_tm - 1)], 0)
+    sent(squares.at[pl.ds(0, n_z - 1)], 0)
+    sent(halves_own.at[0], 5)
 
     @pl.when(owns)
     def _():
-        sent(packed.at[pl.ds(0, 8 * (TILES - 1))], 1)
+        sent(plane_rows.at[pl.ds(0, TILES - 1)], 1)
+        sent(plane_halves.at[pl.ds(0, TILES - 1)], 4)
         sent(ring_rows.at[pl.ds(0, n_z - 1)], 2)
-        sent(plane_rows.at[pl.ds(0, n_plane - 1)], 3)
+        sent(plane_rows.at[pl.ds(0, n_plane - 1), 0], 3)
 
     @pl.when(jnp.logical_not(owns))
     def _():
-        sent(packed.at[pl.ds(0, 8 * TILES)], 1)
-
-
-def finish(grad_ref, total_ref, latent_ref, up_ref, inner_ref, outer_ref, out_ref):
-    latent_ref[0] = grad_ref[...]
+        sent(plane_rows.at[pl.ds(0, TILES)], 1)
+        sent(plane_halves.at[pl.ds(0, TILES)], 4)
+
+
+def finish(grad_ref, total_ref, latent_ref, up_ref, inner_ref, outer_ref, out_ref, store_sem):
+    store = pltpu.make_async_copy(grad_ref, latent_ref.at[0], store_sem)
+    store.start()
     sums = total_ref[...]
     square = jnp.sum(sums * sums, keepdims=True)
     factor = jnp.minimum(1.0, lax.rsqrt(square / PARAMS + 1e-06))
@@ -708,6 +735,7 @@
         inner_ref[j] = sums[64:80, 32 * j : 32 * j + 32]
     outer_ref[...] = sums[64:80, 96:128]
     out_ref[...] = sums[80:87, 0:32]
+    store.wait()
 
 
 def local(n_dp, n_tm, latent, target, up_kernel, inner_kernel, outer_kernel, out_kernel):
@@ -720,7 +748,7 @@
     vmem = pl.BlockSpec(memory_space=pltpu.VMEM)
     grad, total = pl.pallas_call(
         functools.partial(kernel, n_dp, n_tm),
-        out_shape=(shape((64, frames), F32), shape((8 * TILES, 128), F32)),
+        out_shape=(pltpu.VMEM((64, frames), F32), pltpu.VMEM((8 * TILES, 128), F32)),
         in_specs=[hbm] * 9,
         out_specs=(vmem, vmem),
         scratch_shapes=[
@@ -740,31 +768,37 @@
             pltpu.VMEM((24, 256), F32),
             pltpu.VMEM((4, 16, 256), F32),
             pltpu.VMEM((3, 8, 256), F32),
-            pltpu.VMEM((n_tm, 1, 128), F32),
-            pltpu.VMEM((8 * TILES, 128), F32),
+            pltpu.VMEM((n_z, 1, 128), F32),
             pltpu.VMEM((3, 8 * TILES, 128), F32),
             pltpu.VMEM((3, 64, frames), F32),
-            pltpu.VMEM((n_plane, 8, 128), F32),
+            pltpu.VMEM((2, 1, 128), F32),
+            pltpu.VMEM((n_plane, 1, 128), F32),
+            pltpu.VMEM((n_plane, 3, 8, 128), F32),
             pltpu.VMEM((n_z, 8, 128), F32),
             pltpu.SemaphoreType.DMA((9,)),
             pltpu.SemaphoreType.DMA((6,)),
             pltpu.SemaphoreType.DMA((6,)),
-            pltpu.SemaphoreType.DMA((4,)),
-            pltpu.SemaphoreType.DMA((4,)),
+            pltpu.SemaphoreType.DMA((6,)),
+            pltpu.SemaphoreType.DMA((6,)),
         ],
         compiler_params=pltpu.CompilerParams(
-            collective_id=0, has_side_effects=True, vmem_limit_bytes=60 * 1024 * 1024
+            collective_id=0, has_side_effects=True, vmem_limit_bytes=32 * 1024 * 1024
         ),
     )(
-        latent,
-        target,
-        up_kernel,
-        inner_kernel,
-        outer_kernel.T,
-        out_kernel,
-        jnp.asarray(dft),
-        jnp.asarray(mels),
-        jnp.asarray(tapers),
+        *(
+            pltpu.with_memory_space_constraint(x, pltpu.HBM)
+            for x in (
+                latent,
+                target,
+                up_kernel,
+                inner_kernel,
+                outer_kernel.T,
+                out_kernel,
+                jnp.asarray(dft),
+                jnp.asarray(mels),
+                jnp.asarray(tapers),
+            )
+        )
     )
     grad, up, inner, outer, out = pl.pallas_call(
         finish,
@@ -776,8 +810,9 @@
             shape((7, 32), F32),
         ),
         in_specs=[vmem] * 2,
-        out_specs=(vmem,) * 5,
-    )(grad, total)
+        out_specs=(hbm, vmem, vmem, vmem, vmem),
+        scratch_shapes=[pltpu.SemaphoreType.DMA],
+    )(*(pltpu.with_memory_space_constraint(x, pltpu.VMEM) for x in (grad, total)))
     return grad, up, inner, outer.T, out
 
 

time: 58.2 us -> 54.5 us (0.936)
  Pallas kernels: 57.4 us -> 53.8 us
    pallas_call x1, Pallas kernels: 55.6 us -> 52.5 us  [local(): pl.pallas_call(functools.partial(kernel, n_dp, n_tm), out_shape=(pltpu.VM...]
where the time goes in v4:
time: 54.5 us; the launch traced here: 54.4 us
  Pallas kernels  53.8 us (99%)
  between operations  0.64 us (1%)
    pallas_call x1, Pallas kernels, local(): pl.pallas_call(functools.partial(kernel, n_dp, n_tm), out_shape=(pltpu.VM...  52.5 us
    pallas_call x1, Pallas kernels, local(): pl.pallas_call(finish, out_shape=(shape(latent.shape, F32), shape((4, 32,...  1.31 us

profile of v4, /device:TPU:1, one launch (start us, length us, event | category | flops | bytes accessed | tf_op | source)
XLA Modules:
  0.0 54.4 jit_solution(17700229961078072257)
XLA Ops:
  0.6 52.5 %shard_map.128 = (f32[64,512]{1,0:T(8,128)S(1)}, f32[88,128]{1,0:T(8,128)S(1)}) custom-call(f32[1,64,512]{2,1,0:T(8,128)} %latent_hbm.1, f32[1,1024]{1,0:T(1,128)} %target_hbm.1, f32[4,32,64]{2,1,0:T(8,128)} %up_hbm.1, f32[3,16,32]{2,1,0:T(8,128)} %inner_hbm.1, f32[16,32]{1,0:T(8,128)} %bitcast.2, f32[7,32]{1,0:T(8,128)} %out_hbm.1, ...), custom_call_target="tpu_custom_call" | custom-call | tf_op jit(solution)/shard_map/pallas_call | solution.py:749
  53.1 1.3 %shard_map.129 = (f32[1,64,512]{2,1,0:T(8,128)}, f32[4,32,64]{2,1,0:T(8,128)}, f32[3,16,32]{2,1,0:T(8,128)}, f32[16,32]{1,0:T(8,128)}, f32[7,32]{1,0:T(8,128)}) custom-call(f32[64,512]{1,0:T(8,128)S(1)} %get-tuple-element.12.grad_ref, f32[88,128]{1,0:T(8,128)S(1)} %get-tuple-element.13.total_ref), custom_call_target="tpu_custom_call" | custom-call | tf_op jit(solution)/shard_map/pallas_call | solution.py:803

commit v5 on v4

--- a/solution.py
+++ b/solution.py
@@ -219,6 +219,7 @@
     frame_grads,
     grad_blocks,
     squares,
+    window,
     packed_rows,
     grad_rows,
     halves_own,
@@ -244,66 +245,6 @@
     first = tm == 0
     last = tm == n_tm - 1
 
-    barrier = pltpu.get_barrier_semaphore()
-
-    def owner_of(index):
-        return (index * n_plane) // TILES
-
-    def tile_of(member):
-        return (member * TILES + n_plane - 1) // n_plane
-
-    def is_owner(member):
-        index = tile_of(member)
-        return (index < TILES) & (owner_of(index) == member)
-
-    def along_z(i):
-        half = (i + 1) // 2
-        return lax.rem(z + n_z // 2 + half - 2 * half * lax.rem(i, 2) + n_z, n_z)
-
-    def in_plane(visit):
-        core, x, y_lo = lax.rem(dp, 2), lax.rem(dp // 2, 4), dp // 8
-        for dx in (2, 1, 3, 0):
-
-            @pl.loop(0, 8 if dx else 7)
-            def _(i):
-                bits = 7 - i
-                y = lax.rem(y_hi + bits // 4, 2)
-                y_in = lax.rem(y_lo + lax.rem(bits // 2, 2), 2)
-                side = lax.rem(core + lax.rem(bits, 2), 2)
-                visit(y * n_dp + y_in * 8 + lax.rem(x + dx, 4) * 2 + side)
-
-    def member_id(member):
-        return (lax.rem(member, n_dp), (member // n_dp) * n_z + z)
-
-    owns = is_owner(plane)
-    partner = lax.rem(y_hi + 1, Y_HI) * n_dp + dp
-
-    def greet(device):
-        pl.semaphore_signal(barrier, inc=1, device_id=device, device_id_type=MESH)
-
-    @pl.loop(0, n_z - 1)
-    def _(i):
-        greet((dp, y_hi * n_z + along_z(i)))
-
-    greet((dp, other))
-
-    @pl.when(z == n_z - 1)
-    def _():
-        greet((dp, right))
-
-    @pl.when(z == 0)
-    def _():
-        greet((dp, left))
-
-    def greet_member(member):
-        @pl.when((owns | is_owner(member)) & (member != partner))
-        def _():
-            greet(member_id(member))
-
-    in_plane(greet_member)
-    greeted = n_z + jnp.where((z == 0) | (z == n_z - 1), 1, 0)
-    greeted += jnp.where(owns, n_plane - 2, TILES - jnp.where(is_owner(partner), 1, 0))
-
     loads = [
         pltpu.make_async_copy(source, place, load_sem.at[i])
         for i, (source, place) in enumerate(
@@ -325,6 +266,114 @@
     frames = latent.shape[1]
     wide = frames + 128
 
+    barrier = pltpu.get_barrier_semaphore()
+
+    def owner_of(index):
+        return (index * n_plane) // TILES
+
+    def tile_of(member):
+        return (member * TILES + n_plane - 1) // n_plane
+
+    def is_owner(member):
+        index = tile_of(member)
+        return (index < TILES) & (owner_of(index) == member)
+
+    def along_z(i):
+        half = (i + 1) // 2
+        return lax.rem(z + n_z // 2 + half - 2 * half * lax.rem(i, 2) + n_z, n_z)
+
+    def in_plane(visit):
+        core, x, y_lo = lax.rem(dp, 2), lax.rem(dp // 2, 4), dp // 8
+        for dx in (2, 1, 3, 0):
+
+            @pl.loop(0, 8 if dx else 7)
+            def _(i):
+                bits = 7 - i
+                y = lax.rem(y_hi + bits // 4, 2)
+                y_in = lax.rem(y_lo + lax.rem(bits // 2, 2), 2)
+                side = lax.rem(core + lax.rem(bits, 2), 2)
+                visit(y * n_dp + y_in * 8 + lax.rem(x + dx, 4) * 2 + side)
+
+    def member_id(member):
+        return (lax.rem(member, n_dp), (member // n_dp) * n_z + z)
+
+    owns = is_owner(plane)
+    partner = lax.rem(y_hi + 1, Y_HI) * n_dp + dp
+
+    def greet(device):
+        pl.semaphore_signal(barrier, inc=1, device_id=device, device_id_type=MESH)
+
+    reach = n_z // 4
+
+    def beside(i):
+        step = reach - i // 2
+        ahead = z + n_z + step - 2 * step * lax.rem(i, 2)
+        return (dp, y_hi * n_z + lax.rem(ahead, n_z))
+
+    @pl.loop(0, 2 * reach)
+    def _(i):
+        greet(beside(i))
+
+    greet((dp, other))
+
+    @pl.when(z == n_z - 1)
+    def _():
+        greet((dp, right))
+
+    @pl.when(z == 0)
+    def _():
+        greet((dp, left))
+
+    for i in range(TILES):
+        owner = owner_of(i)
+
+        @pl.when((plane != owner) & (partner != owner))
+        def _():
+            greet(member_id(owner))
+
+    @pl.when(owns)
+    def _():
+        def greet_member(member):
+            @pl.when(jnp.logical_not(is_owner(member)) & (member != partner))
+            def _():
+                greet(member_id(member))
+
+        in_plane(greet_member)
+
+    greeted = 2 * reach + 1 + jnp.where((z == 0) | (z == n_z - 1), 1, 0)
+    greeted += jnp.where(owns, n_plane - 2, TILES - jnp.where(is_owner(partner), 1, 0))
+
+    loads[0].wait()
+    lane_8 = lax.broadcasted_iota(jnp.int32, (8, 128), 1)
+    lent = jnp.zeros((8, 128), F32)
+    for g in range(8):
+        start = latent[8 * g : 8 * g + 8, 0:128]
+        end = latent[8 * g : 8 * g + 8, frames - 128 : frames]
+        lent = jnp.where(lane_8 // 4 == g, roll(start, 4 * g), lent)
+        lent = jnp.where(lane_8 // 4 == 16 + g, roll(end, 4 * g - 60), lent)
+    halo[1] = lent
+
+    pl.semaphore_wait(barrier, greeted)
+
+    def send(source, place, slot, device):
+        copy = pltpu.make_async_remote_copy(
+            src_ref=source,
+            dst_ref=place,
+            send_sem=near_send.at[slot],
+            recv_sem=near_recv.at[slot],
+            device_id=device,
+            device_id_type=MESH,
+        )
+        copy.start()
+        return copy
+
+    near = [
+        send(halo.at[1], halo.at[0], 0, (dp, right)),
+        send(halo.at[1], halo.at[2], 1, (dp, left)),
+        send(target_hbm, target_rows.at[0], 2, (dp, right)),
+        send(target_hbm, target_rows.at[2], 3, (dp, left)),
+    ]
+
     loads[2].wait()
     loads[3].wait()
     loads[4].wait()
@@ -376,37 +425,6 @@
     out_w16 = jnp.concatenate([out_w, jnp.zeros((8, 64), F32)], axis=0)
     out_fwd = split(out_w16)
     out_bwd = split(out_w16.T)
-
-    loads[0].wait()
-    lane_8 = lax.broadcasted_iota(jnp.int32, (8, 128), 1)
-    lent = jnp.zeros((8, 128), F32)
-    for g in range(8):
-        start = latent[8 * g : 8 * g + 8, 0:128]
-        end = latent[8 * g : 8 * g + 8, frames - 128 : frames]
-        lent = jnp.where(lane_8 // 4 == g, roll(start, 4 * g), lent)
-        lent = jnp.where(lane_8 // 4 == 16 + g, roll(end, 4 * g - 60), lent)
-    halo[1] = lent
-
-    pl.semaphore_wait(barrier, greeted)
-
-    def send(source, place, slot, device):
-        copy = pltpu.make_async_remote_copy(
-            src_ref=source,
-            dst_ref=place,
-            send_sem=near_send.at[slot],
-            recv_sem=near_recv.at[slot],
-            device_id=device,
-            device_id_type=MESH,
-        )
-        copy.start()
-        return copy
-
-    near = [
-        send(halo.at[1], halo.at[0], 0, (dp, right)),
-        send(halo.at[1], halo.at[2], 1, (dp, left)),
-        send(target_hbm, target_rows.at[0], 2, (dp, right)),
-        send(target_hbm, target_rows.at[2], 3, (dp, left)),
-    ]
 
     lane = lax.broadcasted_iota(jnp.int32, (1, wide), 1)
     inside = (
@@ -576,9 +594,9 @@
     def sent(ref, slot):
         pltpu.make_async_copy(ref, ref, far_send.at[slot]).wait()
 
-    @pl.loop(0, n_z - 1)
+    @pl.loop(0, 2 * reach)
     def _(i):
-        far(squares.at[z], squares.at[z], 0, (dp, y_hi * n_z + along_z(i))).start()
+        far(squares.at[z], squares.at[z], 0, beside(i)).start()
 
     grad_blocks[0] = timed
     grad_blocks[1] = coarse
@@ -638,10 +656,27 @@
         def _():
             far(chunk, plane_rows.at[plane], 1, member_id(owner)).start()
 
-    arrived(squares.at[pl.ds(0, n_z - 1)], 0)
-    sums = squares[0]
-    for i in range(1, n_z):
-        sums = sums + squares[i]
+    arrived(squares.at[pl.ds(0, 2 * reach)], 0)
+
+    def added(first, count):
+        row = squares[lax.rem(z + n_z + first, n_z)]
+        for k in range(1, count):
+            row = row + squares[lax.rem(z + n_z + first + k, n_z)]
+        return row
+
+    ahead, back = added(1, reach), added(1 - reach, reach - 1)
+    window[0] = ahead
+    window[1] = back
+    below, above = (
+        (dp, y_hi * n_z + lax.rem(z + n_z - reach, n_z)),
+        (dp, y_hi * n_z + lax.rem(z + reach, n_z)),
+    )
+    far(window.at[0], window.at[2], 6, below).start()
+    far(window.at[1], window.at[3], 7, above).start()
+    sums = squares[z] + added(-reach, 1) + back + ahead
+    arrived(window.at[2], 6)
+    arrived(window.at[3], 7)
+    sums = sums + window[2] + window[3]
     halves_own[0] = sums
     for i in range(TILES):
         owner = owner_of(i)
@@ -704,7 +739,9 @@
 
     for copy in near:
         copy.wait_send()
-    sent(squares.at[pl.ds(0, n_z - 1)], 0)
+    sent(squares.at[pl.ds(0, 2 * reach)], 0)
+    sent(window.at[0], 6)
+    sent(window.at[1], 7)
     sent(halves_own.at[0], 5)
 
     @pl.when(owns)
@@ -769,6 +806,7 @@
             pltpu.VMEM((4, 16, 256), F32),
             pltpu.VMEM((3, 8, 256), F32),
             pltpu.VMEM((n_z, 1, 128), F32),
+            pltpu.VMEM((4, 1, 128), F32),
             pltpu.VMEM((3, 8 * TILES, 128), F32),
             pltpu.VMEM((3, 64, frames), F32),
             pltpu.VMEM((2, 1, 128), F32),
@@ -778,8 +816,8 @@
             pltpu.SemaphoreType.DMA((9,)),
             pltpu.SemaphoreType.DMA((6,)),
             pltpu.SemaphoreType.DMA((6,)),
-            pltpu.SemaphoreType.DMA((6,)),
-            pltpu.SemaphoreType.DMA((6,)),
+            pltpu.SemaphoreType.DMA((8,)),
+            pltpu.SemaphoreType.DMA((8,)),
         ],
         compiler_params=pltpu.CompilerParams(
             collective_id=0, has_side_effects=True, vmem_limit_bytes=32 * 1024 * 1024

time: 54.5 us -> 54.2 us (level)
  no operation moved by 1% of the time
where the time goes in v5:
time: 54.2 us; the launch traced here: 54 us
  Pallas kernels  53.4 us (99%)
  between operations  0.64 us (1%)
    pallas_call x1, Pallas kernels, local(): pl.pallas_call(functools.partial(kernel, n_dp, n_tm), out_shape=(pltpu.VM...  52.1 us
    pallas_call x1, Pallas kernels, local(): pl.pallas_call(finish, out_shape=(shape(latent.shape, F32), shape((4, 32,...  1.31 us

profile of v5, /device:TPU:1, one launch (start us, length us, event | category | flops | bytes accessed | tf_op | source)
XLA Modules:
  0.0 54.0 jit_solution(4570160640559702587)
XLA Ops:
  0.6 52.1 %shard_map.128 = (f32[64,512]{1,0:T(8,128)S(1)}, f32[88,128]{1,0:T(8,128)S(1)}) custom-call(f32[1,64,512]{2,1,0:T(8,128)} %latent_hbm.1, f32[1,1024]{1,0:T(1,128)} %target_hbm.1, f32[4,32,64]{2,1,0:T(8,128)} %up_hbm.1, f32[3,16,32]{2,1,0:T(8,128)} %inner_hbm.1, f32[16,32]{1,0:T(8,128)} %bitcast.2, f32[7,32]{1,0:T(8,128)} %out_hbm.1, ...), custom_call_target="tpu_custom_call" | custom-call | tf_op jit(solution)/shard_map/pallas_call | solution.py:786
  52.7 1.3 %shard_map.129 = (f32[1,64,512]{2,1,0:T(8,128)}, f32[4,32,64]{2,1,0:T(8,128)}, f32[3,16,32]{2,1,0:T(8,128)}, f32[16,32]{1,0:T(8,128)}, f32[7,32]{1,0:T(8,128)}) custom-call(f32[64,512]{1,0:T(8,128)S(1)} %get-tuple-element.12.grad_ref, f32[88,128]{1,0:T(8,128)S(1)} %get-tuple-element.13.total_ref), custom_call_target="tpu_custom_call" | custom-call | tf_op jit(solution)/shard_map/pallas_call | solution.py:841

commit v6 on v5

--- a/solution.py
+++ b/solution.py
@@ -219,7 +219,6 @@
     frame_grads,
     grad_blocks,
     squares,
-    window,
     packed_rows,
     grad_rows,
     halves_own,
@@ -231,6 +230,8 @@
     near_recv,
     far_send,
     far_recv,
+    known_sem,
+    ready_sem,
 ):
     dp = lax.axis_index("dp")
     tm = lax.axis_index("tm")
@@ -331,17 +332,8 @@
         def _():
             greet(member_id(owner))
 
-    @pl.when(owns)
-    def _():
-        def greet_member(member):
-            @pl.when(jnp.logical_not(is_owner(member)) & (member != partner))
-            def _():
-                greet(member_id(member))
-
-        in_plane(greet_member)
-
     greeted = 2 * reach + 1 + jnp.where((z == 0) | (z == n_z - 1), 1, 0)
-    greeted += jnp.where(owns, n_plane - 2, TILES - jnp.where(is_owner(partner), 1, 0))
+    greeted += jnp.where(owns, n_plane - 2, 0)
 
     loads[0].wait()
     lane_8 = lax.broadcasted_iota(jnp.int32, (8, 128), 1)
@@ -373,6 +365,18 @@
         send(target_hbm, target_rows.at[0], 2, (dp, right)),
         send(target_hbm, target_rows.at[2], 3, (dp, left)),
     ]
+
+    def tell(semaphore, device):
+        pl.semaphore_signal(semaphore, inc=1, device_id=device, device_id_type=MESH)
+
+    below = (dp, y_hi * n_z + lax.rem(z + n_z - reach, n_z))
+    above = (dp, y_hi * n_z + lax.rem(z + reach, n_z))
+    tell(known_sem, below)
+    tell(known_sem, above)
+
+    @pl.when(owns)
+    def _():
+        in_plane(lambda member: tell(ready_sem, member_id(member)))
 
     loads[2].wait()
     loads[3].wait()
@@ -594,9 +598,11 @@
     def sent(ref, slot):
         pltpu.make_async_copy(ref, ref, far_send.at[slot]).wait()
 
-    @pl.loop(0, 2 * reach)
+    pl.semaphore_wait(known_sem, 2)
+
+    @pl.loop(0, n_z - 1)
     def _(i):
-        far(squares.at[z], squares.at[z], 0, beside(i)).start()
+        far(squares.at[z], squares.at[z], 0, (dp, y_hi * n_z + along_z(i))).start()
 
     grad_blocks[0] = timed
     grad_blocks[1] = coarse
@@ -643,6 +649,7 @@
         after = jnp.concatenate([grad_upper, roll(grad_upper, -1)], axis=0)
         grad_rows[i] = weight_dot(up_bwd, after[:, :frames]) * slope_in[:, :frames]
 
+    pl.semaphore_wait(ready_sem, jnp.where(owns, TILES - 1, TILES))
     for i in range(TILES):
         owner = owner_of(i)
         chunk = packed_rows.at[:, pl.ds(8 * i, 8)]
@@ -656,27 +663,10 @@
         def _():
             far(chunk, plane_rows.at[plane], 1, member_id(owner)).start()
 
-    arrived(squares.at[pl.ds(0, 2 * reach)], 0)
-
-    def added(first, count):
-        row = squares[lax.rem(z + n_z + first, n_z)]
-        for k in range(1, count):
-            row = row + squares[lax.rem(z + n_z + first + k, n_z)]
-        return row
-
-    ahead, back = added(1, reach), added(1 - reach, reach - 1)
-    window[0] = ahead
-    window[1] = back
-    below, above = (
-        (dp, y_hi * n_z + lax.rem(z + n_z - reach, n_z)),
-        (dp, y_hi * n_z + lax.rem(z + reach, n_z)),
-    )
-    far(window.at[0], window.at[2], 6, below).start()
-    far(window.at[1], window.at[3], 7, above).start()
-    sums = squares[z] + added(-reach, 1) + back + ahead
-    arrived(window.at[2], 6)
-    arrived(window.at[3], 7)
-    sums = sums + window[2] + window[3]
+    arrived(squares.at[pl.ds(0, n_z - 1)], 0)
+    sums = squares[0]
+    for i in range(1, n_z):
+        sums = sums + squares[i]
     halves_own[0] = sums
     for i in range(TILES):
         owner = owner_of(i)
@@ -739,9 +729,7 @@
 
     for copy in near:
         copy.wait_send()
-    sent(squares.at[pl.ds(0, 2 * reach)], 0)
-    sent(window.at[0], 6)
-    sent(window.at[1], 7)
+    sent(squares.at[pl.ds(0, n_z - 1)], 0)
     sent(halves_own.at[0], 5)
 
     @pl.when(owns)
@@ -806,7 +794,6 @@
             pltpu.VMEM((4, 16, 256), F32),
             pltpu.VMEM((3, 8, 256), F32),
             pltpu.VMEM((n_z, 1, 128), F32),
-            pltpu.VMEM((4, 1, 128), F32),
             pltpu.VMEM((3, 8 * TILES, 128), F32),
             pltpu.VMEM((3, 64, frames), F32),
             pltpu.VMEM((2, 1, 128), F32),
@@ -816,8 +803,10 @@
             pltpu.SemaphoreType.DMA((9,)),
             pltpu.SemaphoreType.DMA((6,)),
             pltpu.SemaphoreType.DMA((6,)),
-            pltpu.SemaphoreType.DMA((8,)),
-            pltpu.SemaphoreType.DMA((8,)),
+            pltpu.SemaphoreType.DMA((6,)),
+            pltpu.SemaphoreType.DMA((6,)),
+            pltpu.SemaphoreType.REGULAR,
+            pltpu.SemaphoreType.REGULAR,
         ],
         compiler_params=pltpu.CompilerParams(
             collective_id=0, has_side_effects=True, vmem_limit_bytes=32 * 1024 * 1024

time: 54.2 us -> 52.2 us (0.963)
  Pallas kernels: 53.4 us -> 51.4 us
    pallas_call x1, Pallas kernels: 52.1 us -> 50.1 us  [local(): pl.pallas_call(functools.partial(kernel, n_dp, n_tm), out_shape=(pltpu.VM...]
where the time goes in v6:
time: 52.2 us; the launch traced here: 52 us
  Pallas kernels  51.4 us (98%)
  between operations  0.64 us (1%)
    pallas_call x1, Pallas kernels, local(): pl.pallas_call(functools.partial(kernel, n_dp, n_tm), out_shape=(pltpu.VM...  50.1 us
    pallas_call x1, Pallas kernels, local(): pl.pallas_call(finish, out_shape=(shape(latent.shape, F32), shape((4, 32,...  1.31 us

profile of v6, /device:TPU:1, one launch (start us, length us, event | category | flops | bytes accessed | tf_op | source)
XLA Modules:
  0.0 52.0 jit_solution(16836801047124492154)
XLA Ops:
  0.6 50.1 %shard_map.128 = (f32[64,512]{1,0:T(8,128)S(1)}, f32[88,128]{1,0:T(8,128)S(1)}) custom-call(f32[1,64,512]{2,1,0:T(8,128)} %latent_hbm.1, f32[1,1024]{1,0:T(1,128)} %target_hbm.1, f32[4,32,64]{2,1,0:T(8,128)} %up_hbm.1, f32[3,16,32]{2,1,0:T(8,128)} %inner_hbm.1, f32[16,32]{1,0:T(8,128)} %bitcast.2, f32[7,32]{1,0:T(8,128)} %out_hbm.1, ...), custom_call_target="tpu_custom_call" | custom-call | tf_op jit(solution)/shard_map/pallas_call | solution.py:774
  50.7 1.3 %shard_map.129 = (f32[1,64,512]{2,1,0:T(8,128)}, f32[4,32,64]{2,1,0:T(8,128)}, f32[3,16,32]{2,1,0:T(8,128)}, f32[16,32]{1,0:T(8,128)}, f32[7,32]{1,0:T(8,128)}) custom-call(f32[64,512]{1,0:T(8,128)S(1)} %get-tuple-element.12.grad_ref, f32[88,128]{1,0:T(8,128)S(1)} %get-tuple-element.13.total_ref), custom_call_target="tpu_custom_call" | custom-call | tf_op jit(solution)/shard_map/pallas_call | solution.py:830

commit v7 on v6

--- a/solution.py
+++ b/solution.py
@@ -230,8 +230,8 @@
     near_recv,
     far_send,
     far_recv,
-    known_sem,
-    ready_sem,
+    near_sem,
+    far_sem,
 ):
     dp = lax.axis_index("dp")
     tm = lax.axis_index("tm")
@@ -299,23 +299,24 @@
         return (lax.rem(member, n_dp), (member // n_dp) * n_z + z)
 
     owns = is_owner(plane)
-    partner = lax.rem(y_hi + 1, Y_HI) * n_dp + dp
 
     def greet(device):
         pl.semaphore_signal(barrier, inc=1, device_id=device, device_id_type=MESH)
 
-    reach = n_z // 4
-
-    def beside(i):
-        step = reach - i // 2
-        ahead = z + n_z + step - 2 * step * lax.rem(i, 2)
-        return (dp, y_hi * n_z + lax.rem(ahead, n_z))
-
-    @pl.loop(0, 2 * reach)
-    def _(i):
-        greet(beside(i))
-
-    greet((dp, other))
+    def shifted_z(by):
+        return (dp, y_hi * n_z + lax.rem(z + n_z + by, n_z))
+
+    core, column, y_lo = lax.rem(dp, 2), lax.rem(dp // 2, 4), dp // 8
+    others_in_y = [
+        (lax.rem(y_lo + in_lo, 2) * 8 + 2 * column + core, lax.rem(y_hi + in_hi, 2) * n_z + z)
+        for in_lo, in_hi in ((0, 1), (1, 1), (1, 0))
+    ]
+    for by in (2, -2, 1, -1):
+        greet(shifted_z(by))
+    for device in others_in_y:
+        greet(device)
+    for dx, side in ((2, 1), (2, 0), (1, 1), (3, 1), (1, 0), (3, 0), (0, 1)):
+        greet((y_lo * 8 + lax.rem(column + dx, 4) * 2 + lax.rem(core + side, 2), tm))
 
     @pl.when(z == n_z - 1)
     def _():
@@ -325,15 +326,7 @@
     def _():
         greet((dp, left))
 
-    for i in range(TILES):
-        owner = owner_of(i)
-
-        @pl.when((plane != owner) & (partner != owner))
-        def _():
-            greet(member_id(owner))
-
-    greeted = 2 * reach + 1 + jnp.where((z == 0) | (z == n_z - 1), 1, 0)
-    greeted += jnp.where(owns, n_plane - 2, 0)
+    greeted = 14 + jnp.where((z == 0) | (z == n_z - 1), 1, 0)
 
     loads[0].wait()
     lane_8 = lax.broadcasted_iota(jnp.int32, (8, 128), 1)
@@ -369,14 +362,8 @@
     def tell(semaphore, device):
         pl.semaphore_signal(semaphore, inc=1, device_id=device, device_id_type=MESH)
 
-    below = (dp, y_hi * n_z + lax.rem(z + n_z - reach, n_z))
-    above = (dp, y_hi * n_z + lax.rem(z + reach, n_z))
-    tell(known_sem, below)
-    tell(known_sem, above)
-
-    @pl.when(owns)
-    def _():
-        in_plane(lambda member: tell(ready_sem, member_id(member)))
+    for device in (shifted_z(2), shifted_z(-2), *others_in_y):
+        tell(near_sem, device)
 
     loads[2].wait()
     loads[3].wait()
@@ -480,6 +467,10 @@
         send(wave_tiles.at[1], wave_tiles.at[2], 5, (dp, left)),
     ]
 
+    pl.semaphore_wait(near_sem, 5)
+    tell(far_sem, shifted_z(4))
+    tell(far_sem, shifted_z(-4))
+
     for load in (loads[1], loads[6], loads[7], loads[8]):
         load.wait()
     near[2].wait_recv()
@@ -598,7 +589,7 @@
     def sent(ref, slot):
         pltpu.make_async_copy(ref, ref, far_send.at[slot]).wait()
 
-    pl.semaphore_wait(known_sem, 2)
+    pl.semaphore_wait(far_sem, 2)
 
     @pl.loop(0, n_z - 1)
     def _(i):
@@ -649,7 +640,6 @@
         after = jnp.concatenate([grad_upper, roll(grad_upper, -1)], axis=0)
         grad_rows[i] = weight_dot(up_bwd, after[:, :frames]) * slope_in[:, :frames]
 
-    pl.semaphore_wait(ready_sem, jnp.where(owns, TILES - 1, TILES))
     for i in range(TILES):
         owner = owner_of(i)
         chunk = packed_rows.at[:, pl.ds(8 * i, 8)]

time: 52.2 us -> 52.1 us (level)
  no operation moved by 1% of the time
where the time goes in v7:
time: 52.1 us; the launch traced here: 51.9 us
  Pallas kernels  51.3 us (98%)
  between operations  0.64 us (1%)
    pallas_call x1, Pallas kernels, local(): pl.pallas_call(functools.partial(kernel, n_dp, n_tm), out_shape=(pltpu.VM...  50 us
    pallas_call x1, Pallas kernels, local(): pl.pallas_call(finish, out_shape=(shape(latent.shape, F32), shape((4, 32,...  1.31 us

profile of v7, /device:TPU:1, one launch (start us, length us, event | category | flops | bytes accessed | tf_op | source)
XLA Modules:
  0.0 51.9 jit_solution(9098287352090851471)
XLA Ops:
  0.6 50.0 %shard_map.128 = (f32[64,512]{1,0:T(8,128)S(1)}, f32[88,128]{1,0:T(8,128)S(1)}) custom-call(f32[1,64,512]{2,1,0:T(8,128)} %latent_hbm.1, f32[1,1024]{1,0:T(1,128)} %target_hbm.1, f32[4,32,64]{2,1,0:T(8,128)} %up_hbm.1, f32[3,16,32]{2,1,0:T(8,128)} %inner_hbm.1, f32[16,32]{1,0:T(8,128)} %bitcast.2, f32[7,32]{1,0:T(8,128)} %out_hbm.1, ...), custom_call_target="tpu_custom_call" | custom-call | tf_op jit(solution)/shard_map/pallas_call | solution.py:764
  50.6 1.3 %shard_map.129 = (f32[1,64,512]{2,1,0:T(8,128)}, f32[4,32,64]{2,1,0:T(8,128)}, f32[3,16,32]{2,1,0:T(8,128)}, f32[16,32]{1,0:T(8,128)}, f32[7,32]{1,0:T(8,128)}) custom-call(f32[64,512]{1,0:T(8,128)S(1)} %get-tuple-element.12.grad_ref, f32[88,128]{1,0:T(8,128)S(1)} %get-tuple-element.13.total_ref), custom_call_target="tpu_custom_call" | custom-call | tf_op jit(solution)/shard_map/pallas_call | solution.py:820

commit v8 on v7

--- a/solution.py
+++ b/solution.py
@@ -66,16 +66,23 @@
     dft = np.concatenate(
         [high, low, fine_high, fine_low, move.astype(ml_dtypes.bfloat16)], axis=0
     )
+    both = np.concatenate([real, imag], axis=1).T
+    back_high, back_low = halves(
+        np.concatenate([t0.T, t2.T, both[:, :256], both[:, 256:]], axis=0)
+    )
+    fine_back_high, fine_back_low = halves(fine.T)
+    back = np.concatenate([back_high, back_low, fine_back_high, fine_back_low], axis=0)
     order = np.concatenate([4 * p, 4 * p + 2, 4 * p + 1, 4 * p + 3])
     mels = np.concatenate([mel_bank(1024)[order], mel_bank(256)], axis=0)
     mels = np.concatenate(halves(mels), axis=1)
     taper = 0.5 - 0.5 * np.cos(2.0 * np.pi * (np.arange(4)[:, None] * 256 + place) / 1024)
     taper_fine = 0.5 - 0.5 * np.cos(2.0 * np.pi * place[None, :] / 256)
     tapers = np.concatenate([taper, taper_fine, np.zeros((3, 256))], axis=0).astype(np.float32)
-    return dft, mels, tapers
+    return dft, back, mels, tapers
 
 
 HIGH, LOW, FINE_HIGH, FINE_LOW, MOVE, ROWS = 0, 1536, 3072, 3328, 3584, 3840
+BACK_ROWS = 3584
 
 
 def split(x):
@@ -99,11 +106,11 @@
     return both[:m] + both[m:] + dot(high, xl)
 
 
-def rows_dot(x, high, low, product=dot):
+def rows_dot(x, high, low):
     m = x.shape[0]
     xh, xl = split(x)
-    both = product(jnp.concatenate([xh, xl], axis=0), high)
-    return both[:m] + both[m:] + product(xh, low)
+    both = dot(jnp.concatenate([xh, xl], axis=0), high)
+    return both[:m] + both[m:] + dot(xh, low)
 
 
 def gram(a, b):
@@ -200,6 +207,7 @@
     dft_hbm,
     mels_hbm,
     tapers_hbm,
+    back_hbm,
     grad_out,
     total,
     latent,
@@ -212,6 +220,7 @@
     table,
     mels,
     tapers,
+    back_table,
     natural,
     target_blocks,
     wave_tiles,
@@ -259,6 +268,7 @@
                 (dft_hbm, table),
                 (mels_hbm, mels),
                 (tapers_hbm, tapers),
+                (back_hbm, back_table),
             ]
         )
     ]
@@ -494,6 +504,8 @@
     s = s * s
     target_fine = level_of(s[:, :128] + s[:, 128:], bank_fine)
 
+    loads[9].wait()
+
     wave_blocks[...] = jnp.zeros(wave_blocks.shape, F32)
     near[4].wait_recv()
     near[5].wait_recv()
@@ -515,22 +527,15 @@
     twice = functools.partial(jnp.concatenate, axis=1)
     d0 = s0 * twice([slope[:, 0:128]] * 2)
     d2 = s2 * twice([slope[:, 128:256]] * 2)
-    d_even = rows_dot(d0, table[HIGH : HIGH + 256, :], table[LOW : LOW + 256, :], dot_nt)
-    d_odd = rows_dot(
-        d2, table[HIGH + 256 : HIGH + 512, :], table[LOW + 256 : LOW + 512, :], dot_nt
-    )
-    d_cross = rows_dot(
-        re * slope[:, 256:512],
-        table[HIGH + 512 : HIGH + 1024, :],
-        table[LOW + 512 : LOW + 1024, :],
-        dot_nt,
-    ) + rows_dot(
-        im * slope[:, 256:512],
-        table[HIGH + 1024 : HIGH + 1536, :],
-        table[LOW + 1024 : LOW + 1536, :],
-        dot_nt,
-    )
-    d_first, d_second = d_cross[:, :256], d_cross[:, 256:]
+    across = twice([re * slope[:, 256:512], im * slope[:, 256:512]])
+
+    def backed(x, start):
+        high, low = HIGH + start, LOW + start
+        depth = x.shape[1]
+        return rows_dot(x, back_table[high : high + depth, :], back_table[low : low + depth, :])
+
+    d_even, d_odd = backed(d0, 0), backed(d2, 256)
+    d_first, d_second = backed(across, 512), backed(across, 1024)
     both, apart = d_even + d_odd, d_even - d_odd
     for b, d in enumerate((both + d_first, apart + d_second, both - d_first, apart - d_second)):
         frame_grads[b] = d * tapers[b : b + 1, :]
@@ -547,9 +552,8 @@
     slope = energy_slope(level, target_fine, valid, bank_fine)
     d = rows_dot(
         spectrum * twice([slope] * 2),
-        table[FINE_HIGH : FINE_HIGH + 256, :],
-        table[FINE_LOW : FINE_LOW + 256, :],
-        dot_nt,
+        back_table[FINE_HIGH : FINE_HIGH + 256, :],
+        back_table[FINE_LOW : FINE_LOW + 256, :],
     )
     d = d * tapers[4:5, :]
     fine = []
@@ -754,7 +758,7 @@
 
 
 def local(n_dp, n_tm, latent, target, up_kernel, inner_kernel, outer_kernel, out_kernel):
-    dft, mels, tapers = tables()
+    dft, back, mels, tapers = tables()
     frames = latent.shape[2]
     n_z = n_tm // Y_HI
     n_plane = n_dp * Y_HI
@@ -764,7 +768,7 @@
     grad, total = pl.pallas_call(
         functools.partial(kernel, n_dp, n_tm),
         out_shape=(pltpu.VMEM((64, frames), F32), pltpu.VMEM((8 * TILES, 128), F32)),
-        in_specs=[hbm] * 9,
+        in_specs=[hbm] * 10,
         out_specs=(vmem, vmem),
         scratch_shapes=[
             pltpu.VMEM((64, frames), F32),
@@ -777,6 +781,7 @@
             pltpu.VMEM((ROWS, 256), BF16),
             pltpu.VMEM((640, 128), BF16),
             pltpu.VMEM((8, 256), F32),
+            pltpu.VMEM((BACK_ROWS, 256), BF16),
             pltpu.VMEM((16, 256), F32),
             pltpu.VMEM((24, 256), F32),
             pltpu.VMEM((3, 8, 128), F32),
@@ -790,7 +795,7 @@
             pltpu.VMEM((n_plane, 1, 128), F32),
             pltpu.VMEM((n_plane, 3, 8, 128), F32),
             pltpu.VMEM((n_z, 8, 128), F32),
-            pltpu.SemaphoreType.DMA((9,)),
+            pltpu.SemaphoreType.DMA((10,)),
             pltpu.SemaphoreType.DMA((6,)),
             pltpu.SemaphoreType.DMA((6,)),
             pltpu.SemaphoreType.DMA((6,)),
@@ -814,6 +819,7 @@
                 jnp.asarray(dft),
                 jnp.asarray(mels),
                 jnp.asarray(tapers),
+                jnp.asarray(back),
             )
         )
     )

time: 52.1 us -> 51.9 us (level)
  no operation moved by 1% of the time
where the time goes in v8:
time: 51.9 us; the launch traced here: 51.7 us
  Pallas kernels  51.1 us (98%)
  between operations  0.64 us (1%)
    pallas_call x1, Pallas kernels, local(): pl.pallas_call(functools.partial(kernel, n_dp, n_tm), out_shape=(pltpu.VM...  49.8 us
    pallas_call x1, Pallas kernels, local(): pl.pallas_call(finish, out_shape=(shape(latent.shape, F32), shape((4, 32,...  1.31 us

profile of v8, /device:TPU:1, one launch (start us, length us, event | category | flops | bytes accessed | tf_op | source)
XLA Modules:
  0.0 51.7 jit_solution(13500079690058808972)
XLA Ops:
  0.6 49.8 %shard_map.137 = (f32[64,512]{1,0:T(8,128)S(1)}, f32[88,128]{1,0:T(8,128)S(1)}) custom-call(f32[1,64,512]{2,1,0:T(8,128)} %latent_hbm.1, f32[1,1024]{1,0:T(1,128)} %target_hbm.1, f32[4,32,64]{2,1,0:T(8,128)} %up_hbm.1, f32[3,16,32]{2,1,0:T(8,128)} %inner_hbm.1, f32[16,32]{1,0:T(8,128)} %bitcast.2, f32[7,32]{1,0:T(8,128)} %out_hbm.1, ...), custom_call_target="tpu_custom_call" | custom-call | tf_op jit(solution)/shard_map/pallas_call | solution.py:768
  50.4 1.3 %shard_map.138 = (f32[1,64,512]{2,1,0:T(8,128)}, f32[4,32,64]{2,1,0:T(8,128)}, f32[3,16,32]{2,1,0:T(8,128)}, f32[16,32]{1,0:T(8,128)}, f32[7,32]{1,0:T(8,128)}) custom-call(f32[64,512]{1,0:T(8,128)S(1)} %get-tuple-element.12.grad_ref, f32[88,128]{1,0:T(8,128)S(1)} %get-tuple-element.13.total_ref), custom_call_target="tpu_custom_call" | custom-call | tf_op jit(solution)/shard_map/pallas_call | solution.py:826

commit v9 on v8

--- a/solution.py
+++ b/solution.py
@@ -692,13 +692,14 @@
     @pl.when(owns)
     def _():
         arrived(plane_rows.at[pl.ds(0, n_plane - 1)], 1)
+        for c in range(n_dp):
+            plane_rows[c] = plane_rows[c] + plane_rows[n_dp + c]
         arrived(plane_halves.at[pl.ds(0, n_plane - 1)], 4)
         chunk = jnp.zeros((8, 128), F32)
         for c in range(n_dp):
             scales = scales_of(plane_halves[c] + plane_halves[n_dp + c])
             for i in range(3):
-                both = plane_rows[c, i] + plane_rows[n_dp + c, i]
-                chunk = chunk + scales[:, i : i + 1] * both
+                chunk = chunk + scales[:, i : i + 1] * plane_rows[c, i]
         ring_rows[z] = chunk
 
         @pl.loop(0, n_z - 1)

time: 51.9 us -> 51.9 us (level)
  no operation moved by 1% of the time
where the time goes in v9:
time: 51.9 us; the launch traced here: 51.7 us
  Pallas kernels  51.1 us (98%)
  between operations  0.64 us (1%)
    pallas_call x1, Pallas kernels, local(): pl.pallas_call(functools.partial(kernel, n_dp, n_tm), out_shape=(pltpu.VM...  49.8 us
    pallas_call x1, Pallas kernels, local(): pl.pallas_call(finish, out_shape=(shape(latent.shape, F32), shape((4, 32,...  1.31 us

profile of v9, /device:TPU:1, one launch (start us, length us, event | category | flops | bytes accessed | tf_op | source)
XLA Modules:
  0.0 51.7 jit_solution(12906460671172549680)
XLA Ops:
  0.6 49.8 %shard_map.137 = (f32[64,512]{1,0:T(8,128)S(1)}, f32[88,128]{1,0:T(8,128)S(1)}) custom-call(f32[1,64,512]{2,1,0:T(8,128)} %latent_hbm.1, f32[1,1024]{1,0:T(1,128)} %target_hbm.1, f32[4,32,64]{2,1,0:T(8,128)} %up_hbm.1, f32[3,16,32]{2,1,0:T(8,128)} %inner_hbm.1, f32[16,32]{1,0:T(8,128)} %bitcast.2, f32[7,32]{1,0:T(8,128)} %out_hbm.1, ...), custom_call_target="tpu_custom_call" | custom-call | tf_op jit(solution)/shard_map/pallas_call | solution.py:769
  50.4 1.3 %shard_map.138 = (f32[1,64,512]{2,1,0:T(8,128)}, f32[4,32,64]{2,1,0:T(8,128)}, f32[3,16,32]{2,1,0:T(8,128)}, f32[16,32]{1,0:T(8,128)}, f32[7,32]{1,0:T(8,128)}) custom-call(f32[64,512]{1,0:T(8,128)S(1)} %get-tuple-element.12.grad_ref, f32[88,128]{1,0:T(8,128)S(1)} %get-tuple-element.13.total_ref), custom_call_target="tpu_custom_call" | custom-call | tf_op jit(solution)/shard_map/pallas_call | solution.py:827
